TPU v7x, 256 devices: a whole 4x4x8 slice. The times are simulated.
256 devices in a mesh: band: 16 (over x, y_lo, core), space: 16 (over y_hi, z).
Axes of the slice: x: 4, y: 4 (y_hi: 2, y_lo: 2; y = y_hi * 2 + y_lo), z: 8, core: 2. Of those that a mesh axis runs over, the one named last changes fastest.
Arguments:
- tokens: bfloat16 [16, 2048, 768], P('band', 'space'), may hold values from -6 to 6
- cotangent: bfloat16 [16, 2048, 768], P('band', 'space'), may hold values from -6 to 6
- visible: int32 [16, 2048], replicated, may hold values 0 or 1
- tau_space: float32 [12], replicated, may hold values from 1 to 48
- tau_band: float32 [12], replicated, may hold values from 1 to 48
- w_qkv_space: bfloat16 [768, 2304], replicated, may hold values from -0.21875 to 0.21875
- w_out_space: bfloat16 [768, 768], replicated, may hold values from -0.21875 to 0.21875
- w_qkv_band: bfloat16 [768, 2304], replicated, may hold values from -0.21875 to 0.21875
- w_out_band: bfloat16 [768, 768], replicated, may hold values from -0.21875 to 0.21875
Outputs:
- mixed: float32 [16, 2048, 768], P('band', 'space')
- input_grad: float32 [16, 2048, 768], P('band', 'space')
All inputs are finite; a program needn't handle non-finite values.
Results may differ from a plain program's by a relative error of at most 0.038.
Values may be sent and summed in bfloat16 or wider, within the bound.
A program may use at most 128 MiB of HBM per device.

v0:
```python
import jax
import jax.numpy as jnp
from jax import lax
from jax.sharding import PartitionSpec as P

D = 768
HEADS = 12
HEAD_DIM = 64
T_DEV = 128
RADIUS = 64
QBLOCK = 128


EPS = 1e-06
NEG_FILL = -1e30


def extended(cells, sides, width):
    for axis, dim in sides:
        count = lax.axis_size(axis)
        head = lax.slice_in_dim(cells, 0, width, axis=dim)
        tail = lax.slice_in_dim(cells, cells.shape[dim] - width, cells.shape[dim], axis=dim)
        cells = jnp.concatenate(
            [
                lax.ppermute(tail, axis, [(i, (i + 1) % count) for i in range(count)]),
                cells,
                lax.ppermute(head, axis, [((i + 1) % count, i) for i in range(count)]),
            ],
            axis=dim,
        )
    return cells


def shifted(value, axis, steps):
    count = lax.axis_size(axis)
    pairs = [(source, (source + steps) % count) for source in range(count)]
    return lax.ppermute(value, axis, pairs)


def row_norm(values):
    factor = lax.rsqrt(jnp.mean(values * values, axis=-1, keepdims=True) + EPS)
    return (values * factor, factor)


def split_heads(tensor):
    return tensor.reshape(tensor.shape[:-1] + (HEADS, HEAD_DIM))


def head_norm(tensor):
    pieces = split_heads(tensor)
    factor = lax.rsqrt(jnp.mean(pieces * pieces, axis=-1, keepdims=True) + EPS)
    return (pieces * factor, factor)


def norm_back(unit, factor, upstream):
    return factor * (upstream - unit * jnp.mean(unit * upstream, axis=-1, keepdims=True))


def project_query(normed, w_qkv):
    return head_norm(jnp.dot(normed, w_qkv[:, :D], preferred_element_type=jnp.float32))


def project_pairs(normed, w_qkv):
    mixed_kv = jnp.dot(normed, w_qkv[:, D:], preferred_element_type=jnp.float32)
    key_unit, key_factor = head_norm(mixed_kv[:, :D])
    return (key_unit, key_factor, split_heads(mixed_kv[:, D:]))


def softmax_masked(scores, allowed):
    scores = jnp.where(allowed, scores, NEG_FILL)
    largest = jnp.max(scores, axis=-1, keepdims=True)
    weights = jnp.where(allowed, jnp.exp(scores - largest), 0.0)
    return (weights / jnp.sum(weights, axis=-1, keepdims=True)).astype(jnp.bfloat16)


def window_weights(query_blk, key_blk, vis_blk, tau):
    query_count = query_blk.shape[0]
    offset = (
        jnp.arange(query_count + 2 * RADIUS, dtype=jnp.int32)[None, :]
        - jnp.arange(query_count, dtype=jnp.int32)[:, None]
    )
    allowed = (
        (offset >= 0) & (offset <= 2 * RADIUS) & ((vis_blk[None, :] == 1) | (offset == RADIUS))
    )
    scores = (
        jnp.einsum("ihd,jhd->hij", query_blk, key_blk, preferred_element_type=jnp.float32)
        * (tau / HEAD_DIM)[:, None, None]
    )
    return softmax_masked(scores, allowed[None])


def window_forward(query_one, key_ext, value_ext, vis_ext, tau):
    weights = window_weights(query_one, key_ext, vis_ext, tau)
    attended = jnp.einsum("hij,jhd->ihd", weights, value_ext, preferred_element_type=jnp.float32)
    pieces = attended.astype(jnp.bfloat16)
    return pieces


def window_backward(query_one, key_ext, value_ext, vis_ext, upstream, tau):
    key_span = QBLOCK + 2 * RADIUS
    grad_key = jnp.zeros(key_ext.shape, jnp.float32)
    grad_value = jnp.zeros(value_ext.shape, jnp.float32)
    weights = window_weights(query_one, key_ext, vis_ext, tau)
    weight_f = weights.astype(jnp.float32)
    dot_weights = jnp.einsum(
        "ihd,jhd->hij", upstream, value_ext, preferred_element_type=jnp.float32
    )
    row_dot = jnp.sum(weight_f * dot_weights, axis=-1, keepdims=True)
    dscore = (weight_f * (dot_weights - row_dot) * (tau / HEAD_DIM)[:, None, None]).astype(
        jnp.bfloat16
    )
    grad_pieces = jnp.einsum("hij,jhd->ihd", dscore, key_ext, preferred_element_type=jnp.float32)
    grad_key = grad_key.at[0:key_span].add(
        jnp.einsum("hij,ihd->jhd", dscore, query_one, preferred_element_type=jnp.float32)
    )
    grad_value = grad_value.at[0:key_span].add(
        jnp.einsum("hij,ihd->jhd", weights, upstream, preferred_element_type=jnp.float32)
    )
    return (grad_pieces, grad_key, grad_value)


def cross_weights(query_two, key_all, allowed, tau):
    scores = (
        jnp.einsum("thd,gthd->thg", query_two, key_all, preferred_element_type=jnp.float32)
        * (tau / HEAD_DIM)[None, :, None]
    )
    return softmax_masked(scores, allowed[:, None, :])


def per_device(
    tokens,
    cotangent,
    visible,
    tau_space,
    tau_band,
    w_qkv_space,
    w_out_space,
    w_qkv_band,
    w_out_band,
):
    band_pos = lax.axis_index("band")
    space_pos = lax.axis_index("space")
    group_count = lax.axis_size("band")
    own_columns = lax.dynamic_slice_in_dim(visible, space_pos * T_DEV, T_DEV, 1)
    group_row = lax.dynamic_index_in_dim(visible, band_pos, 0, keepdims=False)
    vis_ext = jnp.roll(group_row, RADIUS - space_pos * T_DEV)[: T_DEV + 2 * RADIUS]
    inputs = tokens[0].astype(jnp.float32)
    normed_one_unit, normed_one_factor = row_norm(inputs)
    normed_one = normed_one_unit.astype(jnp.bfloat16)
    query_unit, query_factor = project_query(normed_one, w_qkv_space)
    key_unit, key_factor, value_one = project_pairs(normed_one, w_qkv_space)
    joined = jnp.concatenate(
        [
            key_unit.astype(jnp.bfloat16).reshape(T_DEV, D),
            value_one.astype(jnp.bfloat16).reshape(T_DEV, D),
        ],
        axis=1,
    )
    joined_ext = extended(joined, (("space", 0),), RADIUS)
    key_ext = split_heads(joined_ext[:, :D])
    value_ext = split_heads(joined_ext[:, D:])
    query_one = query_unit.astype(jnp.bfloat16)
    attended_one = window_forward(query_one, key_ext, value_ext, vis_ext, tau_space)
    after_one = (
        inputs
        + jnp.dot(attended_one.reshape(T_DEV, D), w_out_space, preferred_element_type=jnp.float32)
    ).astype(jnp.bfloat16)
    after_float = after_one.astype(jnp.float32)
    normed_two_unit, normed_two_factor = row_norm(after_float)
    normed_two = normed_two_unit.astype(jnp.bfloat16)
    upstream_two = cotangent[0]
    grad_att_own = jnp.dot(upstream_two, w_out_band.T, preferred_element_type=jnp.float32).astype(
        jnp.bfloat16
    )
    cross_allowed = (own_columns.T == 1) | (
        jnp.arange(group_count, dtype=jnp.int32)[None, :] == band_pos
    )
    query_two_unit, query_two_factor = project_query(normed_two, w_qkv_band)
    key_two_unit, key_two_factor, value_two = project_pairs(normed_two, w_qkv_band)
    joined_two = jnp.concatenate(
        [
            key_two_unit.astype(jnp.bfloat16).reshape(T_DEV, D),
            value_two.astype(jnp.bfloat16).reshape(T_DEV, D),
        ],
        axis=1,
    )
    gathered = lax.all_gather(joined_two[None], "band", axis=0, tiled=True)
    key_all = split_heads(gathered[:, :, :D])
    value_all = split_heads(gathered[:, :, D:])
    query_two = query_two_unit.astype(jnp.bfloat16)
    cross_w = cross_weights(query_two, key_all, cross_allowed, tau_band)
    attended_two = (
        jnp.einsum("thg,gthd->thd", cross_w, value_all, preferred_element_type=jnp.float32)
        .astype(jnp.bfloat16)
        .reshape(T_DEV, D)
    )
    grad_att_two = split_heads(grad_att_own)
    weight_f = cross_w.astype(jnp.float32)
    dot_weights = jnp.einsum(
        "thd,gthd->thg", grad_att_two, value_all, preferred_element_type=jnp.float32
    )
    row_dot = jnp.sum(weight_f * dot_weights, axis=-1, keepdims=True)
    dscore = (weight_f * (dot_weights - row_dot) * (tau_band / HEAD_DIM)[None, :, None]).astype(
        jnp.bfloat16
    )
    grad_query_two = jnp.einsum(
        "thg,gthd->thd", dscore, key_all, preferred_element_type=jnp.float32
    )
    key_terms = jnp.einsum("thg,thd->gthd", dscore, query_two, preferred_element_type=jnp.float32)
    value_terms = jnp.einsum(
        "thg,thd->gthd", cross_w, grad_att_two, preferred_element_type=jnp.float32
    )
    band_terms = jnp.concatenate(
        [key_terms.reshape(group_count, T_DEV, D), value_terms.reshape(group_count, T_DEV, D)],
        axis=2,
    )
    summed = lax.psum_scatter(
        band_terms.astype(jnp.bfloat16), "band", scatter_dimension=0, tiled=True
    ).astype(jnp.float32)[0]
    grad_key_two = split_heads(summed[:, :D])
    grad_qkv_two = jnp.concatenate(
        [
            norm_back(query_two_unit, query_two_factor, grad_query_two).reshape(T_DEV, D),
            norm_back(key_two_unit, key_two_factor, grad_key_two).reshape(T_DEV, D),
            summed[:, D:],
        ],
        axis=1,
    ).astype(jnp.bfloat16)
    grad_normed_two = jnp.dot(grad_qkv_two, w_qkv_band.T, preferred_element_type=jnp.float32)
    mixed = after_float + jnp.dot(attended_two, w_out_band, preferred_element_type=jnp.float32)
    grad_after = (
        upstream_two.astype(jnp.float32)
        + norm_back(normed_two_unit, normed_two_factor, grad_normed_two)
    ).astype(jnp.bfloat16)
    grad_att_one = split_heads(
        jnp.dot(grad_after, w_out_space.T, preferred_element_type=jnp.float32).astype(jnp.bfloat16)
    )
    grad_query_one, grad_key_ext, grad_value_ext = window_backward(
        query_one, key_ext, value_ext, vis_ext, grad_att_one, tau_space
    )
    rim_terms = jnp.concatenate(
        [
            grad_key_ext.reshape(T_DEV + 2 * RADIUS, D),
            grad_value_ext.reshape(T_DEV + 2 * RADIUS, D),
        ],
        axis=1,
    )
    from_above = shifted(rim_terms[:RADIUS], "space", -1)
    from_below = shifted(rim_terms[T_DEV + RADIUS :], "space", 1)
    own_terms = rim_terms[RADIUS : RADIUS + T_DEV]
    own_terms = own_terms.at[T_DEV - RADIUS :].add(from_above).at[:RADIUS].add(from_below)
    grad_qkv_one = jnp.concatenate(
        [
            norm_back(query_unit, query_factor, grad_query_one).reshape(T_DEV, D),
            norm_back(key_unit, key_factor, split_heads(own_terms[:, :D])).reshape(T_DEV, D),
            own_terms[:, D:],
        ],
        axis=1,
    ).astype(jnp.bfloat16)
    grad_normed_one = jnp.dot(grad_qkv_one, w_qkv_space.T, preferred_element_type=jnp.float32)
    input_grad = grad_after.astype(jnp.float32) + norm_back(
        normed_one_unit, normed_one_factor, grad_normed_one
    )
    return (mixed[None], input_grad[None])


def solution(mesh):
    return jax.shard_map(
        per_device,
        mesh=mesh,
        in_specs=(
            P("band", "space", None),
            P("band", "space", None),
            P(),
            P(),
            P(),
            P(),
            P(),
            P(),
            P(),
        ),
        out_specs=(P("band", "space", None), P("band", "space", None)),
        check_vma=False,
    )
```

profile of v0, /device:TPU:1, one launch (start us, length us, event | category | flops | bytes accessed | tf_op | source)
XLA Modules:
  0.0 278.6 jit_solution(17117191931988181269)
XLA Ops:
  7.2 1.1 fusion.41
  8.4 2.3 fusion.4
  12.9 2.5 collective-permute-start
  15.4 6.6 %collective-permute-start.1 = (bf16[64,1536]{1,0:T(8,128)(2,1)}, bf16[64,1536]{1,0:T(8,128)(2,1)}, u32[]{:S(2)}, u32[]{:S(2)}) collective-permute-start(bf16[64,1536]{1,0:T(8,128)(2,1)} %get-tuple-element.77), channel_id=1, source_target_pairs={{1,0},{2,1},{3,2},{4,3},{5,4},{6,5},{7,6},{8,7},{9,8},{10,9},{11,1... | collective-permute-start | bytes 589832 | tf_op jit(solution)/shard_map/ppermute | solution.py:27
  21.9 1.3 slice_bitcast_fusion
  25.6 1.5 multiply_reduce_fusion.12
  27.2 1.1 pad_maximum_fusion.1
  29.1 1.9 fusion.82
  31.0 1.8 divide_convert_fusion
  35.7 1.1 copy.33
  37.8 1.9 copy.34
  40.8 1.7 pad_maximum_fusion.3
  42.6 1.9 convolution_convert_fusion.1
  45.4 1.2 broadcast_multiply_fusion.4
  46.7 1.4 fusion.68
  48.1 1.9 fusion.10
  50.8 35.8 %all-gather.3.cloned.1.call-done = bf16[2048,1536]{1,0:T(8,128)(2,1)} async-done(((bf16[128,1536]{1,0:T(8,128)(2,1)}), bf16[2048,1536]{1,0:T(8,128)(2,1)}) %all-gather.3.cloned.1.call-update) | async-done | bytes 6291472 | tf_op jit(solution)/shard_map/all_gather | solution.py:187
  86.6 6.1 %fusion.80 = (bf16[16,128,768]{2,1,0:T(8,128)(2,1)}, bf16[16,128,768]{2,1,0:T(8,128)(2,1)}) fusion(bf16[16,128,1536]{2,1,0:T(8,128)(2,1)} %bitcast.120), kind=kLoop, calls=%fused_computation.160 | loop fusion | bytes 12582912 | tf_op jit(solution)/shard_map/slice | solution.py:188
  92.7 4.6 %copy.74 = bf16[16,128,768]{1,2,0:T(8,128)(2,1)} copy(bf16[16,128,768]{2,1,0:T(8,128)(2,1)} %get-tuple-element.68) | data formatting | bytes 6291456
  97.3 4.7 %copy.75 = bf16[16,128,768]{1,2,0:T(8,128)(2,1)} copy(bf16[16,128,768]{2,1,0:T(8,128)(2,1)} %get-tuple-element.69) | data formatting | bytes 6291456
  102.1 5.6 %multiply_reduce_fusion.1 = (f32[128,12,16]{0,1,2:T(8,128)S(1)}, f32[128,12,16]{0,1,2:T(8,128)S(1)}) fusion(bf16[128,12,64,16]{0,2,1,3:T(8,128)(2,1)} %bitcast.110, f32[128,12,64]{0,2,1:T(8,128)} %convert.65, bf16[128,12,64,16]{0,2,1,3:T(8,128)(2,1)} %bitcast.112, f32[128,12,64]{0,2,1:T(8,128)} %fusion.48), kind=kLoop, calls=%fused_computation.4 | loop fusion | flops 9388032 | bytes 7274496 | tf_op jit(solution)/shard_map/thd,gthd->thg/dot_general | solution.py:199
  108.0 2.6 multiply_convert_fusion
  110.7 2.6 multiply_convert_fusion.1
  113.3 4.7 %copy.38 = bf16[16,128,768]{2,1,0:T(8,128)(2,1)} copy(bf16[16,128,768]{1,2,0:T(8,128)(2,1)} %bitcast.115) | data formatting | bytes 6291456 | tf_op jit(solution)/shard_map/reshape | solution.py:214
  118.0 4.7 %copy.39 = bf16[16,128,768]{2,1,0:T(8,128)(2,1)} copy(bf16[16,128,768]{1,2,0:T(8,128)(2,1)} %bitcast.114) | data formatting | bytes 6291456 | tf_op jit(solution)/shard_map/reshape | solution.py:214
  122.7 6.1 %pad_maximum_fusion = bf16[16,128,1536]{2,1,0:T(8,128)(2,1)} fusion(bf16[16,128,768]{2,1,0:T(8,128)(2,1)} %copy.39, bf16[16,128,768]{2,1,0:T(8,128)(2,1)} %copy.38), kind=kLoop, calls=%fused_computation.2 | loop fusion | flops 12582912 | bytes 12582912 | tf_op jit(solution)/shard_map/concatenate | solution.py:213
  128.8 2.7 multiply_reduce_fusion
  132.4 1.8 copy.43
  134.2 2.8 multiply_reduce_fusion.2
  137.0 1.1 fusion.9
  138.1 70.2 %reduce-scatter.2.cloned.1.call-done = bf16[1,128,1536]{2,1,0:T(8,128)(2,1)} async-done(((bf16[16,128,1536]{2,1,0:T(8,128)(2,1)}), bf16[1,128,1536]{2,1,0:T(8,128)(2,1)}) %reduce-scatter.2.cloned.1.call-update) | async-done | bytes 393232 | tf_op jit(solution)/shard_map/reduce_scatter | solution.py:217
  208.3 1.8 slice_convert_fusion.3
  210.1 1.9 copy.40
  212.1 1.1 multiply_reduce_fusion.7
  214.1 1.3 multiply_convert_fusion.4
  215.4 3.4 %multiply_reduce_fusion.6 = (f32[128]{0:T(128)S(1)}, f32[128,768]{1,0:T(8,128)S(1)}) fusion(f32[128,768]{1,0:T(8,128)S(1)} %get-tuple-element.83, f32[128]{0:T(128)} %copy-done.41, bf16[768,2304]{1,0:T(8,128)(2,1)} %param.28, bf16[128,768]{1,0:T(8,128)(2,1)S(1)} %copy-done.32, bf16[128,768]{1,0:T(8,128)(2,1)S(1)} %multiply_convert_fusion.4, ...), kind=kOutput, calls=%fused_computation.89 | convolution fusion | flops 455049088 | bytes 4916224 | tf_op jit(solution)/shard_map/dot_general | solution.py:229
  220.2 1.6 fusion.83
  222.0 3.5 %fusion.15 = f32[12,64,256]{2,1,0:T(8,128)} fusion(bf16[12,128,256]{2,1,0:T(8,128)(2,1)S(1)} %divide_convert_fusion, f32[12,128,256]{2,1,0:T(8,128)} %fusion.83, f32[12]{0:T(128)} %copy-done.47, f32[128,12,64]{0,2,1:T(8,128)} %copy-done.25, f32[128,12]{0,1:T(8,128)S(1)} %copy-done.37), kind=kOutput, calls=%fused_computation.40 | convolution fusion | flops 53282560 | bytes 3545136 | tf_op jit(solution)/shard_map/hij,ihd->jhd/dot_general | solution.py:114
  225.5 1.4 copy.45
  227.7 5.6 %collective-permute-start.2 = (f32[64,1536]{1,0:T(8,128)}, f32[64,1536]{1,0:T(8,128)}, u32[]{:S(2)}, u32[]{:S(2)}) collective-permute-start(f32[64,1536]{1,0:T(8,128)} %fusion.43), channel_id=1, source_target_pairs={{0,15},{1,0},{2,1},{3,2},{4,3},{5,4},{6,5},{7,6},{8,7},{9,8},{10,9... | collective-permute-start | bytes 1179656 | tf_op jit(solution)/shard_map/ppermute | solution.py:37
  234.3 4.1 %multiply_reduce_fusion.5 = (f32[128,12]{0,1:T(8,128)}, f32[128,12,64]{0,2,1:T(8,128)}) fusion(f32[128,12,64]{0,2,1:T(8,128)} %copy-done.25, f32[128,12]{0,1:T(8,128)S(1)} %copy-done.37, bf16[256,12,64]{0,2,1:T(8,128)(2,1)} %bitcast.146, bf16[12,128,256]{2,1,0:T(8,128)(2,1)S(1)} %divide_convert_fusion, f32[12,128,256]{2,1,0:T(8,128)} %fusion.83, ...), kind=kOutput, calls=%fused_computation.87 | convolution fusion | flops 53379328 | bytes 3551280 | tf_op jit(solution)/shard_map/hij,jhd->ihd/dot_general | solution.py:112
  238.4 3.6 %collective-permute-done.2 = f32[64,1536]{1,0:T(8,128)} collective-permute-done((f32[64,1536]{1,0:T(8,128)}, f32[64,1536]{1,0:T(8,128)}, u32[]{:S(2)}, u32[]{:S(2)}) %collective-permute-start.2) | collective-permute-done | bytes 393248 | tf_op jit(solution)/shard_map/ppermute | solution.py:37
  241.9 1.8 pad_maximum_fusion.2
  244.7 14.0 %collective-permute-done.3 = f32[64,1536]{1,0:T(8,128)S(1)} collective-permute-done((f32[64,1536]{1,0:T(8,128)S(1)}, f32[64,1536]{1,0:T(8,128)S(1)}, u32[]{:S(2)}, u32[]{:S(2)}) %collective-permute-start.3) | collective-permute-done | bytes 393248 | tf_op jit(solution)/shard_map/ppermute | solution.py:37
  260.3 2.0 copy.47
  264.1 1.9 copy.48
  266.0 1.1 multiply_convert_fusion.2
  267.2 3.6 %fusion.36 = (f32[128]{0:T(128)S(1)}, f32[128,768]{1,0:T(8,128)S(1)}) fusion(bf16[1,128,768]{2,1,0:T(8,128)(2,1)S(1)} %copy-done.15, f32[128]{0:T(128)S(1)} %copy-done.45, bf16[768,2304]{1,0:T(8,128)(2,1)} %param.26, bf16[128,768]{1,0:T(8,128)(2,1)} %slice.254, bf16[128,768]{1,0:T(8,128)(2,1)S(1)} %multiply_convert_fusion.2, bf16[128,768]{1,0:T(8,128)(2,1)} %copy.50), kind=kOutput, calls=%fused_computation.64 | convolution fusion | flops 455147392 | bytes 4719616 | tf_op jit(solution)/shard_map/dot_general | solution.py:260
  (167 shorter events, 22.5 us)
Async XLA Ops:
  7.2 26.1 %copy-start = (bf16[768,768]{1,0:T(8,128)(2,1)S(1)}, bf16[768,768]{1,0:T(8,128)(2,1)}, u32[]{:S(2)}) copy-start(bf16[768,768]{1,0:T(8,128)(2,1)} %param.27) | copy-start | bytes 3538948
  7.2 79.4 %all-gather.3.cloned.1.call-start = ((), (), s32[]{:S(2)}) async-start(), calls=%async_computation.2 | async-start | bytes 6684672 | tf_op jit(solution)/shard_map/all_gather | solution.py:187
  8.4 2.3 copy-start.44
  10.7 1.3 copy-start.16
  10.7 1.3 copy-start.19
  12.0 10.0 %copy-start.5 = (f32[128,768]{1,0:T(8,128)}, f32[128,768]{1,0:T(8,128)S(1)}, u32[]{:S(2)}) copy-start(f32[128,768]{1,0:T(8,128)S(1)} %copy.28) | copy-start | bytes 1179652
  12.9 14.3 %collective-permute-start = (bf16[64,1536]{1,0:T(8,128)(2,1)}, bf16[64,1536]{1,0:T(8,128)(2,1)}, u32[]{:S(2)}, u32[]{:S(2)}) collective-permute-start(bf16[64,1536]{1,0:T(8,128)(2,1)} %get-tuple-element.76), channel_id=1, source_target_pairs={{0,1},{1,2},{2,3},{3,4},{4,5},{5,6},{6,7},{7,8},{8,9},{9,10},{10,1... | collective-permute-start | bytes 589832 | tf_op jit(solution)/shard_map/ppermute | solution.py:25
  15.4 11.8 %collective-permute-start.1 = (bf16[64,1536]{1,0:T(8,128)(2,1)}, bf16[64,1536]{1,0:T(8,128)(2,1)}, u32[]{:S(2)}, u32[]{:S(2)}) collective-permute-start(bf16[64,1536]{1,0:T(8,128)(2,1)} %get-tuple-element.77), channel_id=1, source_target_pairs={{1,0},{2,1},{3,2},{4,3},{5,4},{6,5},{7,6},{8,7},{9,8},{10,9},{11,1... | collective-permute-start | bytes 589832 | tf_op jit(solution)/shard_map/ppermute | solution.py:27
  25.5 1.6 copy-start.46
  25.6 1.6 copy-start.20
  25.6 1.6 copy-start.22
  27.1 1.7 copy-start.25
  27.1 1.7 copy-start.36
  27.2 1.6 copy-start.47
  28.6 2.4 copy-start.29
  28.8 4.1 %copy-start.12 = (bf16[256,768]{0,1:T(8,128)(2,1)}, bf16[256,768]{0,1:T(8,128)(2,1)S(1)}, u32[]{:S(2)}) copy-start(bf16[256,768]{0,1:T(8,128)(2,1)S(1)} %copy.29) | copy-start | bytes 1179652
  31.0 2.3 copy-start.14
  31.0 2.7 copy-start.11
  36.9 5.6 %copy-start.9 = (f32[128,768]{0,1:T(8,128)}, f32[128,768]{0,1:T(8,128)S(1)}, u32[]{:S(2)}) copy-start(f32[128,768]{0,1:T(8,128)S(1)} %copy.33) | copy-start | bytes 1179652
  37.0 5.5 %copy-start.33 = (f32[128,12]{0,1:T(8,128)}, f32[128,12]{0,1:T(8,128)S(1)}, u32[]{:S(2)}) copy-start(f32[128,12]{0,1:T(8,128)S(1)} %add_rsqrt_fusion) | copy-start | bytes 18436
  42.5 165.8 %reduce-scatter.2.cloned.1.call-start = ((), (), s32[]{:S(2)}) async-start(), calls=%async_computation.1 | async-start | bytes 6684672 | tf_op jit(solution)/shard_map/reduce_scatter | solution.py:217
  42.5 5.5 %copy-start.42 = (f32[128]{0:T(128)S(1)}, f32[128]{0:T(128)}, u32[]{:S(2)}) copy-start(f32[128]{0:T(128)} %copy-done.41) | copy-start | bytes 1540
  102.1 5.6 %copy-start.35 = (pred[128,16]{0,1:T(8,128)(4,1)S(1)}, pred[128,16]{0,1:T(8,128)(4,1)}, u32[]{:S(2)}) copy-start(pred[128,16]{0,1:T(8,128)(4,1)} %fusion.68) | copy-start | bytes 6148
  102.1 5.6 %copy-start.39 = (f32[12]{0:T(128)S(1)}, f32[12]{0:T(128)}, u32[]{:S(2)}) copy-start(f32[12]{0:T(128)} %broadcast_multiply_fusion.4) | copy-start | bytes 148
  102.1 5.9 %copy-start.3 = (f32[128,12,64]{0,2,1:T(8,128)S(1)}, f32[128,12,64]{0,2,1:T(8,128)}, u32[]{:S(2)}) copy-start(f32[128,12,64]{0,2,1:T(8,128)} %convert.65) | copy-start | bytes 1179652
  108.0 2.6 copy-start.18
  108.0 2.7 copy-start.4
  110.7 2.6 copy-start.27
  134.2 2.8 copy-start.2
  137.0 75.1 %copy-start.10 = (f32[128,768]{0,1:T(8,128)S(1)}, f32[128,768]{0,1:T(8,128)}, u32[]{:S(2)}) copy-start(f32[128,768]{0,1:T(8,128)} %copy-done.9) | copy-start | bytes 1179652
  137.0 75.1 %copy-start.34 = (f32[128,12]{0,1:T(8,128)S(1)}, f32[128,12]{0,1:T(8,128)}, u32[]{:S(2)}) copy-start(f32[128,12]{0,1:T(8,128)} %copy-done.33) | copy-start | bytes 18436
  214.1 1.3 copy-start.31
  214.1 1.3 copy-start.32
  215.4 3.5 %copy-start.28 = (bf16[1,128,768]{2,1,0:T(8,128)(2,1)S(1)}, bf16[1,128,768]{2,1,0:T(8,128)(2,1)}, u32[]{:S(2)}) copy-start(bf16[1,128,768]{2,1,0:T(8,128)(2,1)} %param.22) | copy-start | bytes 589828
  215.4 3.5 %copy-start.43 = (f32[128]{0:T(128)S(1)}, f32[128]{0:T(128)}, u32[]{:S(2)}) copy-start(f32[128]{0:T(128)} %copy-done.41) | copy-start | bytes 1540
  220.1 1.8 copy-start.37
  227.7 14.2 %collective-permute-start.2 = (f32[64,1536]{1,0:T(8,128)}, f32[64,1536]{1,0:T(8,128)}, u32[]{:S(2)}, u32[]{:S(2)}) collective-permute-start(f32[64,1536]{1,0:T(8,128)} %fusion.43), channel_id=1, source_target_pairs={{0,15},{1,0},{2,1},{3,2},{4,3},{5,4},{6,5},{7,6},{8,7},{9,8},{10,9... | collective-permute-start | bytes 1179656 | tf_op jit(solution)/shard_map/ppermute | solution.py:37
  238.3 5.4 %copy-start.40 = (f32[128,12]{0,1:T(8,128)S(1)}, f32[128,12]{0,1:T(8,128)}, u32[]{:S(2)}) copy-start(f32[128,12]{0,1:T(8,128)} %get-tuple-element.86) | copy-start | bytes 18436
  238.4 5.5 %copy-start.26 = (f32[128,12,64]{0,2,1:T(8,128)S(1)}, f32[128,12,64]{0,2,1:T(8,128)}, u32[]{:S(2)}) copy-start(f32[128,12,64]{0,2,1:T(8,128)} %copy-done.25) | copy-start | bytes 1179652
  238.4 5.5 %copy-start.30 = (f32[128,12,64]{0,2,1:T(8,128)S(1)}, f32[128,12,64]{0,2,1:T(8,128)}, u32[]{:S(2)}) copy-start(f32[128,12,64]{0,2,1:T(8,128)} %get-tuple-element.87) | copy-start | bytes 1179652
  243.8 14.9 %copy-start.1 = (f32[128,1536]{1,0:T(8,128)S(1)}, f32[128,1536]{1,0:T(8,128)}, u32[]{:S(2)}) copy-start(f32[128,1536]{1,0:T(8,128)} %get-tuple-element.71) | copy-start | bytes 2359300
  243.8 14.9 %collective-permute-start.3 = (f32[64,1536]{1,0:T(8,128)S(1)}, f32[64,1536]{1,0:T(8,128)S(1)}, u32[]{:S(2)}, u32[]{:S(2)}) collective-permute-start(f32[64,1536]{1,0:T(8,128)S(1)} %get-tuple-element.70), channel_id=1, source_target_pairs={{0,1},{1,2},{2,3},{3,4},{4,5},{5,6},{6,7},{7,8},{8,9},{9,10},{10,1... | collective-permute-start | bytes 1179656 | tf_op jit(solution)/shard_map/ppermute | solution.py:37
  258.7 3.6 %copy-start.8 = (f32[128,768]{0,1:T(8,128)S(1)}, f32[128,768]{0,1:T(8,128)}, u32[]{:S(2)}) copy-start(f32[128,768]{0,1:T(8,128)} %copy-done.7) | copy-start | bytes 1179652
  260.3 5.8 %copy-start.6 = (f32[128,768]{1,0:T(8,128)S(1)}, f32[128,768]{1,0:T(8,128)}, u32[]{:S(2)}) copy-start(f32[128,768]{1,0:T(8,128)} %copy-done.5) | copy-start | bytes 1179652
  260.3 5.8 %copy-start.17 = (f32[128,1536]{1,0:T(8,128)S(1)}, f32[128,1536]{1,0:T(8,128)}, u32[]{:S(2)}) copy-start(f32[128,1536]{1,0:T(8,128)} %copy-done.16) | copy-start | bytes 2359300
  263.3 3.8 %copy-start.15 = (bf16[1,128,768]{2,1,0:T(8,128)(2,1)S(1)}, bf16[1,128,768]{2,1,0:T(8,128)(2,1)}, u32[]{:S(2)}) copy-start(bf16[1,128,768]{2,1,0:T(8,128)(2,1)} %param.21) | copy-start | bytes 589828
  263.3 3.8 %copy-start.45 = (f32[128]{0:T(128)S(1)}, f32[128]{0:T(128)}, u32[]{:S(2)}) copy-start(f32[128]{0:T(128)} %copy-done.44) | copy-start | bytes 1540
  267.1 3.6 %copy-start.24 = (bf16[128,768]{1,0:T(8,128)(2,1)S(1)}, bf16[128,768]{1,0:T(8,128)(2,1)}, u32[]{:S(2)}) copy-start(bf16[128,768]{1,0:T(8,128)(2,1)} %copy-done.23) | copy-start | bytes 589828
  (6 other events, 4.8 us)
Sparse Core Ops, SparseCore 0:
  42.6 43.9 all-gather.2
  129.0 79.2 reduce-scatter.1
where the time goes:
time: 280 us; the launch traced here: 279 us
  waiting for transfers between devices  124 us (44%)
  local copies, waits for them, and re-layouts  48.7 us (17%)
  other arithmetic  47.7 us (17%)
  matrix products  29 us (10%)
  between operations  15 us (5%)
  starting transfers between devices  14.7 us (5%)
    reduce_scatter x1, waiting for transfers between devices, per_device(): lax.psum_scatter(band_terms.astype(jnp.bfloat16), 'band', scatter_dimensi...  70.2 us
    all_gather x1, waiting for transfers between devices, per_device(): gathered = lax.all_gather(joined_two[None], 'band', axis=0, tiled=True)  35.8 us
    ppermute x2, waiting for transfers between devices, shifted(): return lax.ppermute(value, axis, pairs)  17.5 us
    unnamed x98, local copies, waits for them, and re-layouts  10.7 us
    another operation x6, other arithmetic  8.44 us
    ppermute x1, starting transfers between devices, extended(): lax.ppermute(head, axis, [((i + 1) % count, i) for i in range(count)])  6.58 us
    slice x1, local copies, waits for them, and re-layouts, per_device(): key_all = split_heads(gathered[:, :, :D])  6.12 us
    concatenate x1, other arithmetic, per_device(): jnp.concatenate([key_terms.reshape(group_count, T_DEV, D), value_terms.re...  6.06 us
  transfers between devices with their start and end apart: 6, of which 4 were waited for; matrix products, arithmetic and copies ran while one was open for 10% of the time, Pallas kernels for 0%

commit v1 on v0

v1 whole, which is shorter than its diff:
```python
import functools

import jax
import jax.numpy as jnp
from jax import lax
from jax.experimental import pallas as pl
from jax.experimental.pallas import tpu as pltpu
from jax.sharding import PartitionSpec as P

D = 768
HALF = D // 2
HEADS = 12
HEAD_DIM = 64
PAIRS = HEADS // 2
T = 128
RADIUS = 64
EPS = 1e-06
MESH = pl.DeviceIdType.MESH
F32 = jnp.float32
BF16 = jnp.bfloat16


def dot(left, right):
    return jnp.dot(left, right, preferred_element_type=F32)


def dot_nt(left, right):
    return lax.dot_general(left, right, (((1,), (1,)), ((), ())), preferred_element_type=F32)


def dot_tn(left, right):
    return lax.dot_general(left, right, (((0,), (0,)), ((), ())), preferred_element_type=F32)


def row_factor(values):
    return lax.rsqrt(jnp.sum(values * values, axis=-1, keepdims=True) * (1.0 / D) + EPS)


def row_back(unit, factor, upstream):
    return factor * (upstream - unit * (jnp.sum(unit * upstream, axis=-1, keepdims=True) * (1.0 / D)))


def head_means(values, ones):
    low = values.astype(BF16)
    width = ones.shape[0]
    parts = [dot(low[:, at : at + width], ones) for at in range(0, values.shape[1], width)]
    return jnp.concatenate(parts, axis=1) * (1.0 / HEAD_DIM)


def head_factor(values, ones):
    return lax.rsqrt(head_means(values * values, ones) + EPS)


def head_back(unit, factor, upstream, ones):
    return factor * (upstream - unit * head_means(unit * upstream, ones))


def stacked(pair, low):
    return jnp.concatenate([jnp.where(low, pair, 0.0), jnp.where(low, 0.0, pair)], axis=0).astype(BF16)


def lanes(pair):
    return slice(pair * 128, pair * 128 + 128)


def pair_weights(query_stack, key_pair, mask, scale_a, scale_b):
    scores = dot_nt(query_stack, key_pair)
    pieces = []
    for part, scale in ((scores[:T], scale_a), (scores[T:], scale_b)):
        grown = jnp.exp(part * scale) * mask
        pieces.append(grown * (1.0 / jnp.sum(grown, axis=-1, keepdims=True)))
    return jnp.concatenate(pieces, axis=0).astype(BF16)


def pair_dscore(weights, upstream_stack, value_pair, scale_a, scale_b):
    inner = dot_nt(upstream_stack, value_pair)
    weight_f = weights.astype(F32)
    pieces = []
    for rows, scale in ((slice(0, T), scale_a), (slice(T, 2 * T), scale_b)):
        w, p = weight_f[rows], inner[rows]
        total = jnp.sum(w * p, axis=-1, keepdims=True)
        pieces.append(w * (p - total) * scale)
    return jnp.concatenate(pieces, axis=0).astype(BF16)


def kernel(
    bands,
    spaces,
    tok_hbm,
    cot_hbm,
    vis_hbm,
    tau_space,
    tau_band,
    wqs_hbm,
    wos_hbm,
    wqb_hbm,
    wob_hbm,
    mixed_ref,
    grad_ref,
    tok,
    halo,
    cot,
    vis,
    wqs,
    wos,
    wqb,
    wob,
    key_ext,
    value_ext,
    query_stack,
    weights_one,
    unit_q,
    fact_q,
    unit_k,
    fact_k,
    wide,
    after,
    grads,
    grad_kv,
    sent,
    got,
    rim_sent,
    rim_got,
    local_sem,
    halo_send,
    halo_recv,
    all_send,
    all_recv,
    rim_send,
    rim_recv,
):
    band = lax.axis_index("band")
    space = lax.axis_index("space")
    count = T // bands
    right = lax.rem(space + 1, spaces)
    left = lax.rem(space + spaces - 1, spaces)

    def local(source, target, index):
        return pltpu.make_async_copy(source, target, local_sem.at[index])

    copies = {
        "tok": local(tok_hbm.at[0], tok, 0),
        "wqs": local(wqs_hbm, wqs, 1),
        "cot": local(cot_hbm.at[0], cot, 2),
        "wos": local(wos_hbm, wos, 3),
        "wob": local(wob_hbm, wob, 4),
        "wqb": local(wqb_hbm, wqb, 5),
    }
    for index, block in enumerate((left, space, right)):
        copies["vis%d" % index] = local(
            vis_hbm.at[:, pl.ds(pl.multiple_of(block * T, T), T)], vis.at[index], 6 + index
        )
    for name in ("tok", "wqs", "cot", "vis0", "vis1", "vis2", "wos", "wob", "wqb"):
        copies[name].start()

    barrier = pltpu.get_barrier_semaphore()
    for step in range(1, bands):
        pl.semaphore_signal(
            barrier,
            inc=1,
            device_id=(lax.rem(band + step, bands), space),
            device_id_type=MESH,
        )
    for other in (left, right):
        pl.semaphore_signal(barrier, inc=1, device_id=(band, other), device_id_type=MESH)
    pl.semaphore_wait(barrier, bands + 1)

    to_right = pltpu.make_async_remote_copy(
        src_ref=tok_hbm.at[0, pl.ds(T - RADIUS, RADIUS)],
        dst_ref=halo.at[pl.ds(RADIUS, RADIUS)],
        send_sem=halo_send.at[0],
        recv_sem=halo_recv.at[0],
        device_id=(band, right),
        device_id_type=MESH,
    )
    to_left = pltpu.make_async_remote_copy(
        src_ref=tok_hbm.at[0, pl.ds(0, RADIUS)],
        dst_ref=halo.at[pl.ds(0, RADIUS)],
        send_sem=halo_send.at[1],
        recv_sem=halo_recv.at[1],
        device_id=(band, left),
        device_id_type=MESH,
    )
    to_right.start()
    to_left.start()

    def exchange(phase, step):
        other = lax.rem(band + step, bands)
        return pltpu.make_async_remote_copy(
            src_ref=sent.at[phase, other],
            dst_ref=got.at[phase, band],
            send_sem=all_send.at[phase, step],
            recv_sem=all_recv.at[phase, step],
            device_id=(other, space),
            device_id_type=MESH,
        )

    def scatter(phase, rows):
        pieces = [
            rows[:, :HALF].reshape(bands, count, HALF),
            rows[:, HALF:].reshape(bands, count, HALF),
        ]
        sent[phase] = jnp.concatenate(pieces, axis=1).astype(BF16)
        for step in range(1, bands):
            exchange(phase, step).start()
        got[phase, band] = sent[phase, band]

    def collect(phase):
        for step in range(1, bands):
            exchange(phase, step).wait_recv()
        rows = got[phase].astype(F32)
        return jnp.concatenate(
            [rows[:, :count].reshape(T, HALF), rows[:, count:].reshape(T, HALF)], axis=1
        )

    low = lax.broadcasted_iota(jnp.int32, (T, 128), 1) < HEAD_DIM
    ones = jnp.where(
        (lax.broadcasted_iota(jnp.int32, (256, 256), 0) >> 6)
        == (lax.broadcasted_iota(jnp.int32, (256, 256), 1) >> 6),
        1.0,
        0.0,
    ).astype(BF16)
    scale_space = [tau_space[head] * (1.0 / HEAD_DIM) for head in range(HEADS)]
    scale_band = [tau_band[head] * (1.0 / HEAD_DIM) for head in range(HEADS)]

    copies["cot"].wait()
    scatter(0, cot[...].astype(F32))

    for index in range(3):
        copies["vis%d" % index].wait()
    group = lax.broadcasted_iota(jnp.int32, (bands, 128), 0)
    lane = lax.broadcasted_iota(jnp.int32, (bands, 128), 1)

    def own_row(index):
        return jnp.sum(jnp.where(group == band, vis[index], 0), axis=0, keepdims=True)

    edge = lane[:1] < RADIUS
    vis_row = jnp.concatenate([own_row(1), jnp.where(edge, own_row(2), own_row(0))], axis=1)
    row = lax.broadcasted_iota(jnp.int32, (T, 2 * T), 0)
    col = lax.broadcasted_iota(jnp.int32, (T, 2 * T), 1)
    offset = jnp.where(col < T + RADIUS, col, col - 2 * T) - row
    near = (offset >= -RADIUS) & (offset <= RADIUS)
    mask_one = jnp.where(near & ((vis_row == 1) | (offset == 0)), 1.0, 0.0)
    row, col = row[:, :T], col[:, :T]
    pick = jnp.where(row == band * count + lax.rem(col, count), 1.0, 0.0)
    spread = dot(vis[1].astype(F32), pick)
    seen = jnp.sum(
        jnp.where(group == lax.div(lane, count), spread, 0.0), axis=0, keepdims=True
    )
    same = lax.rem(row, count) == lax.rem(col, count)
    mask_two = jnp.where(same & ((seen > 0.5) | (row == col)), 1.0, 0.0)

    copies["tok"].wait()
    inputs = tok[...].astype(F32)
    fact_one = row_factor(inputs)
    unit_one = inputs * fact_one
    normed = unit_one.astype(BF16)
    copies["wqs"].wait()
    raw = dot(normed, wqs[:, :D])
    factor = head_factor(raw, ones)
    unit = raw * factor
    unit_q[0] = unit
    fact_q[0] = factor
    for pair in range(PAIRS):
        query_stack[0, pair] = stacked(unit[:, lanes(pair)], low)
    raw = dot(normed, wqs[:, D : 2 * D])
    factor = head_factor(raw, ones)
    unit = raw * factor
    unit_k[0] = unit
    fact_k[0] = factor
    key_ext[:T] = unit.astype(BF16)
    value_ext[:T] = dot(normed, wqs[:, 2 * D :]).astype(BF16)

    to_right.wait_recv()
    to_left.wait_recv()
    rim = halo[...].astype(F32)
    normed = (rim * row_factor(rim)).astype(BF16)
    raw = dot(normed, wqs[:, D : 2 * D])
    key_ext[T:] = (raw * head_factor(raw, ones)).astype(BF16)
    value_ext[T:] = dot(normed, wqs[:, 2 * D :]).astype(BF16)

    for pair in range(PAIRS):
        weights = pair_weights(
            query_stack[0, pair],
            key_ext[:, lanes(pair)],
            mask_one,
            scale_space[2 * pair],
            scale_space[2 * pair + 1],
        )
        weights_one[pair] = weights
        out = dot(weights, value_ext[:, lanes(pair)])
        wide[:, lanes(pair)] = jnp.where(low, out[:T], out[T:]).astype(BF16)
    copies["wos"].wait()
    result = tok[...].astype(F32) + dot(wide[:, :D], wos[...])
    after[...] = result.astype(BF16)
    scatter(1, after[...].astype(F32))

    upstream = collect(0)
    copies["wob"].wait()
    grad_att = dot_nt(upstream.astype(BF16), wob[...])
    for pair in range(PAIRS):
        query_stack[2, pair] = stacked(grad_att[:, lanes(pair)], low)
    copies["wqb"].wait()
    rows = collect(1)
    fact_two = row_factor(rows)
    unit_two = rows * fact_two
    normed = unit_two.astype(BF16)
    raw = dot(normed, wqb[:, :D])
    factor = head_factor(raw, ones)
    unit = raw * factor
    unit_q[1] = unit
    fact_q[1] = factor
    for pair in range(PAIRS):
        query_stack[1, pair] = stacked(unit[:, lanes(pair)], low)
    raw = dot(normed, wqb[:, D : 2 * D])
    factor = head_factor(raw, ones)
    unit = raw * factor
    unit_k[1] = unit
    fact_k[1] = factor
    key_two = unit.astype(BF16)
    value_two = dot(normed, wqb[:, 2 * D :]).astype(BF16)
    attended = []
    for pair in range(PAIRS):
        scales = (scale_band[2 * pair], scale_band[2 * pair + 1])
        keys, values = key_two[:, lanes(pair)], value_two[:, lanes(pair)]
        queries, ups = query_stack[1, pair], query_stack[2, pair]
        weights = pair_weights(queries, keys, mask_two, *scales)
        out = dot(weights, values)
        attended.append(jnp.where(low, out[:T], out[T:]))
        dscore = pair_dscore(weights, ups, values, *scales)
        out = dot(dscore, keys)
        grads[:, pair * 128 : pair * 128 + 128] = jnp.where(low, out[:T], out[T:])
        grads[:, D + pair * 128 : D + pair * 128 + 128] = dot_tn(dscore, queries)
        wide[:, 2 * D + pair * 128 : 2 * D + pair * 128 + 128] = dot_tn(weights, ups).astype(BF16)
    scatter(2, jnp.concatenate(attended, axis=1))
    wide[:, :D] = head_back(unit_q[1], fact_q[1], grads[:, :D], ones).astype(BF16)
    wide[:, D : 2 * D] = head_back(unit_k[1], fact_k[1], grads[:, D:], ones).astype(BF16)
    back = dot_nt(wide[...], wqb[...])
    scatter(3, upstream + row_back(unit_two, fact_two, back))

    mixed_ref[0] = after[...].astype(F32) + dot(collect(2).astype(BF16), wob[...])
    grad_after = collect(3)
    grad_att = dot_nt(grad_after.astype(BF16), wos[...])
    for pair in range(PAIRS):
        query_stack[2, pair] = stacked(grad_att[:, lanes(pair)], low)

    def rims(pair):
        for side, other in ((0, right), (1, left)):
            yield pltpu.make_async_remote_copy(
                src_ref=rim_sent.at[pair, pl.ds(side * RADIUS, RADIUS)],
                dst_ref=rim_got.at[pair, pl.ds(side * RADIUS, RADIUS)],
                send_sem=rim_send.at[side, pair],
                recv_sem=rim_recv.at[side, pair],
                device_id=(band, other),
                device_id_type=MESH,
            )

    for pair in range(PAIRS):
        scales = (scale_space[2 * pair], scale_space[2 * pair + 1])
        keys, values = key_ext[:, lanes(pair)], value_ext[:, lanes(pair)]
        queries, ups = query_stack[0, pair], query_stack[2, pair]
        weights = weights_one[pair]
        dscore = pair_dscore(weights, ups, values, *scales)
        out = dot_tn(dscore, queries)
        grad_kv[pair, :, :128] = out[:T]
        rim_sent[pair, :, :128] = out[T:].astype(BF16)
        out = dot_tn(weights, ups)
        grad_kv[pair, :, 128:] = out[:T]
        rim_sent[pair, :, 128:] = out[T:].astype(BF16)
        for copy in rims(pair):
            copy.start()
        out = dot(dscore, keys)
        grads[:, pair * 128 : pair * 128 + 128] = jnp.where(low, out[:T], out[T:])
    wide[:, :D] = head_back(unit_q[0], fact_q[0], grads[:, :D], ones).astype(BF16)
    back = dot_nt(wide[:, :D], wqs[:, :D])
    for pair in range(PAIRS):
        for copy in rims(pair):
            copy.wait_recv()
        total = grad_kv[pair] + rim_got[pair].astype(F32)
        grads[:, D + pair * 128 : D + pair * 128 + 128] = total[:, :128]
        wide[:, 2 * D + pair * 128 : 2 * D + pair * 128 + 128] = total[:, 128:].astype(BF16)
    wide[:, D : 2 * D] = head_back(unit_k[0], fact_k[0], grads[:, D:], ones).astype(BF16)
    back = back + dot_nt(wide[:, D:], wqs[:, D:])
    inputs = tok[...].astype(F32)
    fact_one = row_factor(inputs)
    grad_ref[0] = grad_after + row_back(inputs * fact_one, fact_one, back)

    to_right.wait_send()
    to_left.wait_send()
    for phase in range(4):
        for step in range(1, bands):
            exchange(phase, step).wait_send()
    for pair in range(PAIRS):
        for copy in rims(pair):
            copy.wait_send()


def per_device(bands, spaces, *arrays):
    any_space = pl.BlockSpec(memory_space=pl.ANY)
    smem = pl.BlockSpec(memory_space=pltpu.SMEM)
    vmem = pl.BlockSpec(memory_space=pltpu.VMEM)
    out = jax.ShapeDtypeStruct((1, T, D), F32)
    count = T // bands
    dma = pltpu.SemaphoreType.DMA
    scratch = [
        pltpu.VMEM((T, D), BF16),
        pltpu.VMEM((T, D), BF16),
        pltpu.VMEM((T, D), BF16),
        pltpu.VMEM((3, bands, T), jnp.int32),
        pltpu.VMEM((D, 3 * D), BF16),
        pltpu.VMEM((D, D), BF16),
        pltpu.VMEM((D, 3 * D), BF16),
        pltpu.VMEM((D, D), BF16),
        pltpu.VMEM((2 * T, D), BF16),
        pltpu.VMEM((2 * T, D), BF16),
        pltpu.VMEM((3, PAIRS, 2 * T, 128), BF16),
        pltpu.VMEM((PAIRS, 2 * T, 2 * T), BF16),
        pltpu.VMEM((2, T, D), F32),
        pltpu.VMEM((2, T, D), F32),
        pltpu.VMEM((2, T, D), F32),
        pltpu.VMEM((2, T, D), F32),
        pltpu.VMEM((T, 3 * D), BF16),
        pltpu.VMEM((T, D), BF16),
        pltpu.VMEM((T, 2 * D), F32),
        pltpu.VMEM((PAIRS, T, 256), F32),
        pltpu.VMEM((4, bands, 2 * count, HALF), BF16),
        pltpu.VMEM((4, bands, 2 * count, HALF), BF16),
        pltpu.VMEM((PAIRS, T, 256), BF16),
        pltpu.VMEM((PAIRS, T, 256), BF16),
        dma((9,)),
        dma((2,)),
        dma((2,)),
        dma((4, bands)),
        dma((4, bands)),
        dma((2, PAIRS)),
        dma((2, PAIRS)),
    ]
    return pl.pallas_call(
        functools.partial(kernel, bands, spaces),
        out_shape=(out, out),
        in_specs=[any_space] * 3 + [smem] * 2 + [any_space] * 4,
        out_specs=(vmem, vmem),
        scratch_shapes=scratch,
        compiler_params=pltpu.CompilerParams(
            collective_id=0, has_side_effects=True, vmem_limit_bytes=48 * 1024 * 1024
        ),
        cost_estimate=pl.CostEstimate(
            flops=3_500_000_000, bytes_accessed=11_000_000, transcendentals=600_000
        ),
    )(*arrays)


def solution(mesh):
    cells = P("band", "space", None)
    return jax.shard_map(
        functools.partial(per_device, mesh.shape["band"], mesh.shape["space"]),
        mesh=mesh,
        in_specs=(cells, cells, P(), P(), P(), P(), P(), P(), P()),
        out_specs=(cells, cells),
        check_vma=False,
    )
```

time: 280 us -> 57.3 us (0.20)
  waiting for transfers between devices: 124 us -> 0 us
  Pallas kernels: 0 us -> 48.3 us
  other arithmetic: 47.7 us -> 0 us
  local copies, waits for them, and re-layouts: 48.7 us -> 8.09 us
  matrix products: 29 us -> 0 us
  starting transfers between devices: 14.7 us -> 0 us
  between operations: 15 us -> 0.66 us
    reduce_scatter x1 -> x0, waiting for transfers between devices: 70.2 us -> none  [per_device(): lax.psum_scatter(band_terms.astype(jnp.bfloat16), 'band', scatter_dimensi...]
    pallas_call x0 -> x1, Pallas kernels: none -> 48.3 us  [per_device(): pl.pallas_call(functools.partial(kernel, bands, spaces), out_shape=(out,...]
    all_gather x1 -> x0, waiting for transfers between devices: 35.8 us -> none  [per_device(): gathered = lax.all_gather(joined_two[None], 'band', axis=0, tiled=True)]
    dot_general x15 -> x0, matrix products: 27.1 us -> none  [the longest x1 4.06 us: window_backward(): jnp.einsum('hij,jhd->ihd', dscore, key_ext, preferred_element_type=jnp.fl...]
    ppermute x4 -> x0, waiting for transfers between devices: 17.6 us -> none  [the longest x2 17.5 us: shifted(): return lax.ppermute(value, axis, pairs)]
    slice x14 -> x0, local copies, waits for them, and re-layouts: 14.7 us -> none  [the longest x1 6.12 us: per_device(): key_all = split_heads(gathered[:, :, :D])]
    ppermute x4 -> x0, starting transfers between devices: 14.7 us -> none  [the longest x1 6.58 us: extended(): lax.ppermute(head, axis, [((i + 1) % count, i) for i in range(count)])]
    reshape x6 -> x0, local copies, waits for them, and re-layouts: 13.6 us -> none  [the longest x1 4.72 us: per_device(): value_terms.reshape(group_count, T_DEV, D)]
  transfers between devices with their start and end apart: 6 -> 0, of which waited for: 4 -> 0; matrix products, arithmetic and copies ran while one was open for 10% -> 0% of each run, Pallas kernels for 0% -> 0%
where the time goes in v1:
time: 57.3 us; the launch traced here: 57.1 us
  Pallas kernels  48.3 us (84%)
  local copies, waits for them, and re-layouts  8.09 us (14%)
  between operations  0.66 us (1%)
    pallas_call x1, Pallas kernels, per_device(): pl.pallas_call(functools.partial(kernel, bands, spaces), out_shape=(out,...  48.3 us
    unnamed x16, local copies, waits for them, and re-layouts  8.09 us

profile of v1, /device:TPU:1, one launch (start us, length us, event | category | flops | bytes accessed | tf_op | source)
XLA Modules:
  0.0 57.1 jit_solution(8673846451371693942)
XLA Ops:
  0.6 0.0 copy-start
  0.6 1.3 %copy-done = bf16[768,768]{1,0:T(8,128)(2,1)S(1)} copy-done((bf16[768,768]{1,0:T(8,128)(2,1)S(1)}, bf16[768,768]{1,0:T(8,128)(2,1)}, u32[]{:S(2)}) %copy-start) | copy-done | bytes 1179672
  1.9 0.0 copy-start.1
  1.9 1.3 %copy-done.1 = bf16[768,768]{1,0:T(8,128)(2,1)S(1)} copy-done((bf16[768,768]{1,0:T(8,128)(2,1)S(1)}, bf16[768,768]{1,0:T(8,128)(2,1)}, u32[]{:S(2)}) %copy-start.1) | copy-done | bytes 1179672
  3.2 0.0 copy-start.2
  3.2 0.9 %copy-done.2 = bf16[1,128,768]{2,1,0:T(8,128)(2,1)S(1)} copy-done((bf16[1,128,768]{2,1,0:T(8,128)(2,1)S(1)}, bf16[1,128,768]{2,1,0:T(8,128)(2,1)}, u32[]{:S(2)}) %copy-start.2) | copy-done | bytes 196632
  4.1 0.0 copy-start.3
  4.1 0.9 %copy-done.3 = bf16[1,128,768]{2,1,0:T(8,128)(2,1)S(1)} copy-done((bf16[1,128,768]{2,1,0:T(8,128)(2,1)S(1)}, bf16[1,128,768]{2,1,0:T(8,128)(2,1)}, u32[]{:S(2)}) %copy-start.3) | copy-done | bytes 196632
  5.0 0.0 copy-start.4
  5.0 0.9 %copy-done.4 = s32[16,2048]{1,0:T(8,128)S(1)} copy-done((s32[16,2048]{1,0:T(8,128)S(1)}, s32[16,2048]{1,0:T(8,128)}, u32[]{:S(2)}) %copy-start.4) | copy-done | bytes 131096
  5.9 0.0 copy-start.5
  5.9 0.7 %copy-done.5 = f32[12]{0:T(128)S(1)} copy-done((f32[12]{0:T(128)S(1)}, f32[12]{0:T(128)}, u32[]{:S(2)}) %copy-start.5) | copy-done | bytes 72
  6.6 0.0 copy-start.6
  6.6 0.7 %copy-done.6 = f32[12]{0:T(128)S(1)} copy-done((f32[12]{0:T(128)S(1)}, f32[12]{0:T(128)}, u32[]{:S(2)}) %copy-start.6) | copy-done | bytes 72
  7.2 48.3 %shard_map.104 = (f32[1,128,768]{2,1,0:T(8,128)S(1)}, f32[1,128,768]{2,1,0:T(8,128)S(1)}) custom-call(bf16[1,128,768]{2,1,0:T(8,128)(2,1)S(1)} %copy-done.2, bf16[1,128,768]{2,1,0:T(8,128)(2,1)S(1)} %copy-done.3, s32[16,2048]{1,0:T(8,128)S(1)} %copy-done.4, f32[12]{0:T(128)S(1)} %copy-done.5, f32[12]{0:T(128)S(1)} %copy-done.6, bf16[768,2304]{1,0:T(8,128)(2,1)} %wqs_hbm.1, ...), custom_call_target="tpu_custom_call" | custom-call | flops 3500000000 | bytes 11000000 | tf_op jit(solution)/shard_map/pallas_call | solution.py:438
  55.6 0.7 %copy.13 = f32[1,128,768]{2,1,0:T(8,128)} copy(f32[1,128,768]{2,1,0:T(8,128)S(1)} %get-tuple-element.4) | data formatting | bytes 786432
  56.3 0.7 %copy.14 = f32[1,128,768]{2,1,0:T(8,128)} copy(f32[1,128,768]{2,1,0:T(8,128)S(1)} %get-tuple-element.5) | data formatting | bytes 786432
Async XLA Ops:
  0.6 1.3 %copy-start = (bf16[768,768]{1,0:T(8,128)(2,1)S(1)}, bf16[768,768]{1,0:T(8,128)(2,1)}, u32[]{:S(2)}) copy-start(bf16[768,768]{1,0:T(8,128)(2,1)} %wos_hbm.1) | copy-start | bytes 3538948
  1.9 1.3 %copy-start.1 = (bf16[768,768]{1,0:T(8,128)(2,1)S(1)}, bf16[768,768]{1,0:T(8,128)(2,1)}, u32[]{:S(2)}) copy-start(bf16[768,768]{1,0:T(8,128)(2,1)} %wob_hbm.1) | copy-start | bytes 3538948
  3.2 0.9 %copy-start.2 = (bf16[1,128,768]{2,1,0:T(8,128)(2,1)S(1)}, bf16[1,128,768]{2,1,0:T(8,128)(2,1)}, u32[]{:S(2)}) copy-start(bf16[1,128,768]{2,1,0:T(8,128)(2,1)} %tok_hbm.1) | copy-start | bytes 589828
  4.1 0.9 %copy-start.3 = (bf16[1,128,768]{2,1,0:T(8,128)(2,1)S(1)}, bf16[1,128,768]{2,1,0:T(8,128)(2,1)}, u32[]{:S(2)}) copy-start(bf16[1,128,768]{2,1,0:T(8,128)(2,1)} %cot_hbm.1) | copy-start | bytes 589828
  5.0 0.9 %copy-start.4 = (s32[16,2048]{1,0:T(8,128)S(1)}, s32[16,2048]{1,0:T(8,128)}, u32[]{:S(2)}) copy-start(s32[16,2048]{1,0:T(8,128)} %vis_hbm.1) | copy-start | bytes 393220
  5.9 0.7 %copy-start.5 = (f32[12]{0:T(128)S(1)}, f32[12]{0:T(128)}, u32[]{:S(2)}) copy-start(f32[12]{0:T(128)} %tau_space.1) | copy-start | bytes 148
  6.6 0.7 %copy-start.6 = (f32[12]{0:T(128)S(1)}, f32[12]{0:T(128)}, u32[]{:S(2)}) copy-start(f32[12]{0:T(128)} %tau_band.1) | copy-start | bytes 148

commit v2 on v1

v2 whole, which is shorter than its diff:
```python
import functools

import jax
import jax.numpy as jnp
from jax import lax
from jax.experimental import pallas as pl
from jax.experimental.pallas import tpu as pltpu
from jax.sharding import PartitionSpec as P

D = 768
HALF = D // 2
HEADS = 12
HEAD_DIM = 64
PAIRS = HEADS // 2
T = 128
RADIUS = 64
EPS = 1e-06
MESH = pl.DeviceIdType.MESH
F32 = jnp.float32
BF16 = jnp.bfloat16


def dot(left, right):
    return jnp.dot(left, right, preferred_element_type=F32)


def dot_nt(left, right):
    return lax.dot_general(left, right, (((1,), (1,)), ((), ())), preferred_element_type=F32)


def dot_tn(left, right):
    return lax.dot_general(left, right, (((0,), (0,)), ((), ())), preferred_element_type=F32)


def row_factor(values):
    return lax.rsqrt(jnp.sum(values * values, axis=-1, keepdims=True) * (1.0 / D) + EPS)


def row_back(unit, factor, upstream):
    return factor * (upstream - unit * (jnp.sum(unit * upstream, axis=-1, keepdims=True) * (1.0 / D)))


def head_means(values, ones):
    low = values.astype(BF16)
    width = ones.shape[0]
    parts = [dot(low[:, at : at + width], ones) for at in range(0, values.shape[1], width)]
    return jnp.concatenate(parts, axis=1) * (1.0 / HEAD_DIM)


def head_factor(values, ones):
    return lax.rsqrt(head_means(values * values, ones) + EPS)


def head_back(unit, factor, upstream, ones):
    return factor * (upstream - unit * head_means(unit * upstream, ones))


def stacked(pair, low):
    return jnp.concatenate([jnp.where(low, pair, 0.0), jnp.where(low, 0.0, pair)], axis=0).astype(BF16)


def lanes(pair):
    return slice(pair * 128, pair * 128 + 128)


def paired(low, stack):
    return jnp.where(low, stack[:T], stack[T:])


def grown(query_stack, keys, mask):
    scores = jnp.exp(dot_nt(query_stack, keys))
    return jnp.concatenate([scores[:T] * mask, scores[T:] * mask], axis=0).astype(BF16)


def inner(ups, outs, values_one):
    return dot_nt(jnp.concatenate([ups, outs], axis=1), values_one)


def kernel(
    bands,
    spaces,
    tok_hbm,
    cot_hbm,
    vis_hbm,
    tau_space_hbm,
    tau_band_hbm,
    wqs_hbm,
    wos_hbm,
    wqb_hbm,
    wob_hbm,
    mixed_hbm,
    grad_hbm,
    tok,
    halo,
    cot,
    vis,
    tau_space,
    tau_band,
    wqs,
    wos,
    wqb,
    wob,
    wqs_t,
    wos_t,
    wqb_t,
    keys,
    values,
    keys_two,
    values_two,
    queries,
    ups_stack,
    grown_one,
    grown_rim,
    partial,
    inverse,
    inverse_rim,
    unit_q,
    fact_q,
    unit_k,
    fact_k,
    wide,
    after,
    attended,
    attended_rim,
    stats,
    stats_rim,
    grads,
    sent,
    got,
    got_rim,
    mixed,
    grad,
    local_sem,
    near_send,
    near_recv,
    all_send,
    all_recv,
    far_send,
    far_recv,
):
    band = lax.axis_index("band")
    space = lax.axis_index("space")
    count = T // bands
    right = lax.rem(space + 1, spaces)
    left = lax.rem(space + spaces - 1, spaces)

    def local(source, target, index):
        return pltpu.make_async_copy(source, target, local_sem.at[index])

    copies = {
        "tok": local(tok_hbm.at[0], tok, 0),
        "wqs": local(wqs_hbm, wqs, 1),
        "cot": local(cot_hbm.at[0], cot, 2),
        "wos": local(wos_hbm, wos, 3),
        "wob": local(wob_hbm, wob, 4),
        "wqb": local(wqb_hbm, wqb, 5),
        "tau_space": local(tau_space_hbm, tau_space, 9),
        "tau_band": local(tau_band_hbm, tau_band, 10),
        "mixed": local(mixed, mixed_hbm.at[0], 11),
        "grad": local(grad, grad_hbm.at[0], 12),
    }
    for index, block in enumerate((left, space, right)):
        copies["vis%d" % index] = local(
            vis_hbm.at[:, pl.ds(pl.multiple_of(block * T, T), T)], vis.at[index], 6 + index
        )
    early = ("tok", "cot", "vis0", "vis1", "vis2", "tau_space", "tau_band", "wqs")
    late = ("wob", "wos", "wqb")
    for name in early:
        copies[name].start()

    barrier = pltpu.get_barrier_semaphore()
    for other in (left, right):
        pl.semaphore_signal(barrier, inc=1, device_id=(band, other), device_id_type=MESH)
    for step in range(1, bands):
        pl.semaphore_signal(
            barrier,
            inc=1,
            device_id=(lax.rem(band + step, bands), space),
            device_id_type=MESH,
        )
    pl.semaphore_wait(barrier, bands + 1)

    def neighbours(source, target, index):
        return [
            pltpu.make_async_remote_copy(
                src_ref=source.at[pl.ds(at, RADIUS)],
                dst_ref=target.at[pl.ds(at, RADIUS)],
                send_sem=near_send.at[index, side],
                recv_sem=near_recv.at[index, side],
                device_id=(band, other),
                device_id_type=MESH,
            )
            for side, at, other in ((0, RADIUS, right), (1, 0, left))
        ]

    near = [
        neighbours(tok_hbm.at[0], halo, 0),
        neighbours(attended, attended_rim, 1),
        neighbours(stats, stats_rim, 2),
    ]
    for copy in near[0]:
        copy.start()

    def exchange(phase, step):
        other = lax.rem(band + step, bands)
        return pltpu.make_async_remote_copy(
            src_ref=sent.at[phase, other],
            dst_ref=got.at[phase, band],
            send_sem=all_send.at[phase, step],
            recv_sem=all_recv.at[phase, step],
            device_id=(other, space),
            device_id_type=MESH,
        )

    def scatter(phase, rows):
        pieces = [
            rows[:, :HALF].reshape(bands, count, HALF),
            rows[:, HALF:].reshape(bands, count, HALF),
        ]
        sent[phase] = jnp.concatenate(pieces, axis=1).astype(BF16)
        for step in range(1, bands):
            exchange(phase, step).start()
        got[phase, band] = sent[phase, band]

    def unpacked(slots):
        rows = slots.astype(F32)
        return jnp.concatenate(
            [rows[:, :count].reshape(T, HALF), rows[:, count:].reshape(T, HALF)], axis=1
        )

    def collect(phase):
        for step in range(1, bands):
            exchange(phase, step).wait_recv()
        return unpacked(got[phase])

    toward = lax.rem(space + spaces - 1 + 2 * lax.div(band, bands // 2), spaces)

    def far(step):
        other = lax.rem(band + step, bands)
        return pltpu.make_async_remote_copy(
            src_ref=sent.at[3, other],
            dst_ref=got_rim.at[band],
            send_sem=far_send.at[step],
            recv_sem=far_recv.at[band],
            device_id=(other, toward),
            device_id_type=MESH,
        )

    def far_arrival(sender):
        return pltpu.make_async_remote_copy(
            src_ref=sent.at[3, sender],
            dst_ref=got_rim.at[sender],
            send_sem=far_send.at[sender],
            recv_sem=far_recv.at[sender],
            device_id=(band, toward),
            device_id_type=MESH,
        )

    low = lax.broadcasted_iota(jnp.int32, (T, 128), 1) < HEAD_DIM
    ones = jnp.where(
        (lax.broadcasted_iota(jnp.int32, (256, 256), 0) >> 6)
        == (lax.broadcasted_iota(jnp.int32, (256, 256), 1) >> 6),
        1.0,
        0.0,
    ).astype(BF16)
    for pair in range(PAIRS):
        values[pair, :, 128:] = jnp.ones((2 * T, 128), BF16)
        values_two[pair, :, 128:] = jnp.ones((T, 128), BF16)

    copies["cot"].wait()
    scatter(0, cot[...].astype(F32))

    for index in range(3):
        copies["vis%d" % index].wait()
    group = lax.broadcasted_iota(jnp.int32, (bands, 128), 0)
    lane = lax.broadcasted_iota(jnp.int32, (bands, 128), 1)

    def own_row(index):
        return jnp.sum(jnp.where(group == band, vis[index], 0), axis=0, keepdims=True)

    row = lax.broadcasted_iota(jnp.int32, (T, T), 0)
    col = lax.broadcasted_iota(jnp.int32, (T, T), 1)
    own_seen = own_row(1) == 1
    rim_seen = jnp.where(lane[:1] < RADIUS, own_row(2), own_row(0)) == 1

    def within(offset):
        return (offset >= -RADIUS) & (offset <= RADIUS)

    def flag(test):
        return jnp.where(test, 1.0, 0.0)

    mask_own = flag(within(row - col) & (own_seen | (row == col)))
    mask_rim = flag(within(jnp.where(col < RADIUS, col + T, col - T) - row) & rim_seen)
    mask_back = flag(within(jnp.where(row < RADIUS, row + T, row - T) - col) & own_seen)
    pick = flag(row == band * count + lax.rem(col, count))
    spread = dot(vis[1].astype(F32), pick)
    seen = jnp.sum(
        jnp.where(group == lax.div(lane, count), spread, 0.0), axis=0, keepdims=True
    )
    same = lax.rem(row, count) == lax.rem(col, count)
    mask_two = flag(same & ((seen > 0.5) | (row == col)))

    copies["tau_space"].wait()
    copies["tau_band"].wait()

    def scale_row(tau):
        pieces = [
            jnp.where(low[:1], tau[2 * pair], tau[2 * pair + 1]) * (1.0 / HEAD_DIM)
            for pair in range(PAIRS)
        ]
        return jnp.concatenate(pieces, axis=1)

    scale_space = scale_row(tau_space)
    scale_band = scale_row(tau_band)

    def put_queries(slot, unit, scale):
        scaled = unit * scale
        for pair in range(PAIRS):
            queries[slot, pair] = stacked(scaled[:, lanes(pair)], low)

    def normed_heads(normed, weight, slot, which):
        raw = dot(normed, weight)
        factor = head_factor(raw, ones)
        unit = raw * factor
        if which is not None:
            which[0][slot] = unit
            which[1][slot] = factor
        return unit

    copies["tok"].wait()
    inputs = tok[...].astype(F32)
    normed = (inputs * row_factor(inputs)).astype(BF16)
    copies["wqs"].wait()
    for name in late:
        copies[name].start()
    put_queries(0, normed_heads(normed, wqs[:, :D], 0, (unit_q, fact_q)), scale_space)
    keys[:T] = normed_heads(normed, wqs[:, D : 2 * D], 0, (unit_k, fact_k)).astype(BF16)
    raw = dot(normed, wqs[:, 2 * D :]).astype(BF16)
    for pair in range(PAIRS):
        values[pair, :T, :128] = raw[:, lanes(pair)]
    for pair in range(PAIRS):
        weight = grown(queries[0, pair], keys[:T, lanes(pair)], mask_own)
        grown_one[pair, :, :T] = weight
        partial[pair] = dot(weight, values[pair, :T])

    for copy in near[0]:
        copy.wait_recv()
    rim = halo[...].astype(F32)
    normed = (rim * row_factor(rim)).astype(BF16)
    keys[T:] = normed_heads(normed, wqs[:, D : 2 * D], None, None).astype(BF16)
    raw = dot(normed, wqs[:, 2 * D :]).astype(BF16)
    for pair in range(PAIRS):
        values[pair, T:, :128] = raw[:, lanes(pair)]
    table = jnp.zeros((T, 128), F32)
    for pair in range(PAIRS):
        weight = grown(queries[0, pair], keys[T:, lanes(pair)], mask_rim)
        grown_one[pair, :, T:] = weight
        out = partial[pair] + dot(weight, values[pair, T:])
        turned = 1.0 / out[:, 128:]
        inverse[0, pair] = turned
        attended[:, lanes(pair)] = paired(low, out[:, :128] * turned).astype(BF16)
        table = jnp.where(col == 2 * pair, turned[:T], table)
        table = jnp.where(col == 2 * pair + 1, turned[T:], table)
    stats[...] = table
    copies["wos"].wait()
    after[...] = (inputs + dot(attended[...], wos[...])).astype(BF16)
    scatter(1, after[...].astype(F32))
    for index in (1, 2):
        for copy in near[index]:
            copy.start()

    upstream = collect(0)
    copies["wob"].wait()
    grad_att = dot_nt(upstream.astype(BF16), wob[...])
    for pair in range(PAIRS):
        ups_stack[pair] = stacked(grad_att[:, lanes(pair)], low)
    put_queries(2, normed_heads(normed, wqs[:, :D], None, None), scale_space)
    copies["wqb"].wait()
    for at in range(0, 3 * D, 256):
        wqb_t[at : at + 256] = wqb[:, at : at + 256].T

    rows = collect(1)
    fact_two = row_factor(rows)
    unit_two = rows * fact_two
    normed = unit_two.astype(BF16)
    put_queries(1, normed_heads(normed, wqb[:, :D], 1, (unit_q, fact_q)), scale_band)
    keys_two[...] = normed_heads(normed, wqb[:, D : 2 * D], 1, (unit_k, fact_k)).astype(BF16)
    raw = dot(normed, wqb[:, 2 * D :]).astype(BF16)
    for pair in range(PAIRS):
        values_two[pair, :, :128] = raw[:, lanes(pair)]
    outs = []
    for pair in range(PAIRS):
        at = lanes(pair)
        query, key, value, ups = queries[1, pair], keys_two[:, at], values_two[pair], ups_stack[pair]
        weight = grown(query, key, mask_two)
        out = dot(weight, value)
        turned = 1.0 / out[:, 128:]
        out = out[:, :128] * turned
        outs.append(paired(low, out))
        ups_f = ups.astype(F32)
        dscore = inner(ups, (-ups_f * out).astype(BF16), value) * turned
        dscore = (weight.astype(F32) * dscore).astype(BF16)
        grads[:, at] = paired(low, dot(dscore, key)) * scale_band[:, at]
        grads[:, D + pair * 128 : D + pair * 128 + 128] = dot_tn(dscore, query)
        wide[:, 2 * D + pair * 128 : 2 * D + pair * 128 + 128] = dot_tn(
            weight, (ups_f * turned).astype(BF16)
        ).astype(BF16)
    wide[:, :D] = head_back(unit_q[1], fact_q[1], grads[:, :D], ones).astype(BF16)
    wide[:, D : 2 * D] = head_back(unit_k[1], fact_k[1], grads[:, D:], ones).astype(BF16)
    back = dot(wide[...], wqb_t[...])
    scatter(3, upstream + row_back(unit_two, fact_two, back))
    for step in range(bands):
        far(step).start()
    scatter(2, jnp.concatenate(outs, axis=1))

    for at in range(0, 3 * D, 256):
        wqs_t[at : at + 256] = wqs[:, at : at + 256].T
    for at in range(0, D, 256):
        wos_t[at : at + 256] = wos[:, at : at + 256].T
    for index in (1, 2):
        for copy in near[index]:
            copy.wait_recv()
    for pair in range(PAIRS):
        grown_rim[pair] = grown(queries[2, pair], keys[:T, lanes(pair)], mask_back)
        for part in range(2):
            head = 2 * pair + part
            inverse_rim[pair, part * T : part * T + T] = jnp.broadcast_to(
                stats_rim[:, head : head + 1], (T, 128)
            )

    grad_after = collect(3)
    grad_att = dot(grad_after.astype(BF16), wos_t[...])
    for pair in range(PAIRS):
        at = lanes(pair)
        query, value, weight = queries[0, pair], values[pair], grown_one[pair]
        ups_f = jnp.concatenate(
            [jnp.where(low, grad_att[:, at], 0.0), jnp.where(low, 0.0, grad_att[:, at])], axis=0
        )
        out = attended[:, at].astype(F32)
        turned = inverse[0, pair]
        dscore = inner(
            ups_f.astype(BF16),
            (-ups_f * jnp.concatenate([out, out], axis=0)).astype(BF16),
            value,
        )
        dscore = dscore * jnp.concatenate([turned, turned], axis=1)
        dscore = (weight.astype(F32) * dscore).astype(BF16)
        grads[:, at] = paired(low, dot(dscore, keys[:, at])) * scale_space[:, at]
        partial[pair, :T, :128] = dot_tn(dscore[:, :T], query)
        partial[pair, :T, 128:] = dot_tn(weight[:, :T], (ups_f * turned).astype(BF16))
    wide[:, :D] = head_back(unit_q[0], fact_q[0], grads[:, :D], ones).astype(BF16)
    back = dot(wide[:, :D], wqs_t[:D])
    mixed[...] = after[...].astype(F32) + dot(collect(2).astype(BF16), wob[...])
    copies["mixed"].start()

    for sender in range(bands):
        far_arrival(sender).wait_recv()
    grad_att = dot(unpacked(got_rim[...]).astype(BF16), wos_t[...])
    for pair in range(PAIRS):
        at = lanes(pair)
        query, weight, turned = queries[2, pair], grown_rim[pair], inverse_rim[pair]
        ups_f = jnp.concatenate(
            [jnp.where(low, grad_att[:, at], 0.0), jnp.where(low, 0.0, grad_att[:, at])], axis=0
        )
        out = attended_rim[:, at].astype(F32)
        dscore = inner(
            ups_f.astype(BF16),
            (-ups_f * jnp.concatenate([out, out], axis=0)).astype(BF16),
            values[pair, :T],
        )
        dscore = (weight.astype(F32) * (dscore * turned)).astype(BF16)
        grads[:, D + pair * 128 : D + pair * 128 + 128] = partial[pair, :T, :128] + dot_tn(
            dscore, query
        )
        wide[:, 2 * D + pair * 128 : 2 * D + pair * 128 + 128] = (
            partial[pair, :T, 128:] + dot_tn(weight, (ups_f * turned).astype(BF16))
        ).astype(BF16)
    wide[:, D : 2 * D] = head_back(unit_k[0], fact_k[0], grads[:, D:], ones).astype(BF16)
    back = back + dot(wide[:, D:], wqs_t[D:])
    inputs = tok[...].astype(F32)
    fact_one = row_factor(inputs)
    grad[...] = grad_after + row_back(inputs * fact_one, fact_one, back)
    copies["grad"].start()

    for index in range(3):
        for copy in near[index]:
            copy.wait_send()
    for phase in range(4):
        for step in range(1, bands):
            exchange(phase, step).wait_send()
    for step in range(bands):
        far(step).wait_send()
    copies["mixed"].wait()
    copies["grad"].wait()


def per_device(bands, spaces, *arrays):
    hbm = pl.BlockSpec(memory_space=pltpu.HBM)
    out = jax.ShapeDtypeStruct((1, T, D), F32)
    count = T // bands
    dma = pltpu.SemaphoreType.DMA
    scratch = [
        pltpu.VMEM((T, D), BF16),
        pltpu.VMEM((T, D), BF16),
        pltpu.VMEM((T, D), BF16),
        pltpu.VMEM((3, bands, T), jnp.int32),
        pltpu.SMEM((HEADS,), F32),
        pltpu.SMEM((HEADS,), F32),
        pltpu.VMEM((D, 3 * D), BF16),
        pltpu.VMEM((D, D), BF16),
        pltpu.VMEM((D, 3 * D), BF16),
        pltpu.VMEM((D, D), BF16),
        pltpu.VMEM((3 * D, D), BF16),
        pltpu.VMEM((D, D), BF16),
        pltpu.VMEM((3 * D, D), BF16),
        pltpu.VMEM((2 * T, D), BF16),
        pltpu.VMEM((PAIRS, 2 * T, 256), BF16),
        pltpu.VMEM((T, D), BF16),
        pltpu.VMEM((PAIRS, T, 256), BF16),
        pltpu.VMEM((3, PAIRS, 2 * T, 128), BF16),
        pltpu.VMEM((PAIRS, 2 * T, 128), BF16),
        pltpu.VMEM((PAIRS, 2 * T, 2 * T), BF16),
        pltpu.VMEM((PAIRS, 2 * T, T), BF16),
        pltpu.VMEM((PAIRS, 2 * T, 256), F32),
        pltpu.VMEM((1, PAIRS, 2 * T, 128), F32),
        pltpu.VMEM((PAIRS, 2 * T, 128), F32),
        pltpu.VMEM((2, T, D), F32),
        pltpu.VMEM((2, T, D), F32),
        pltpu.VMEM((2, T, D), F32),
        pltpu.VMEM((2, T, D), F32),
        pltpu.VMEM((T, 3 * D), BF16),
        pltpu.VMEM((T, D), BF16),
        pltpu.VMEM((T, D), BF16),
        pltpu.VMEM((T, D), BF16),
        pltpu.VMEM((T, 128), F32),
        pltpu.VMEM((T, 128), F32),
        pltpu.VMEM((T, 2 * D), F32),
        pltpu.VMEM((4, bands, 2 * count, HALF), BF16),
        pltpu.VMEM((4, bands, 2 * count, HALF), BF16),
        pltpu.VMEM((bands, 2 * count, HALF), BF16),
        pltpu.VMEM((T, D), F32),
        pltpu.VMEM((T, D), F32),
        dma((13,)),
        dma((3, 2)),
        dma((3, 2)),
        dma((4, bands)),
        dma((4, bands)),
        dma((bands,)),
        dma((bands,)),
    ]
    return pl.pallas_call(
        functools.partial(kernel, bands, spaces),
        out_shape=(out, out),
        in_specs=[hbm] * 9,
        out_specs=(hbm, hbm),
        scratch_shapes=scratch,
        compiler_params=pltpu.CompilerParams(
            collective_id=0, has_side_effects=True, vmem_limit_bytes=64 * 1024 * 1024 - 65536
        ),
        cost_estimate=pl.CostEstimate(
            flops=3_500_000_000, bytes_accessed=11_000_000, transcendentals=600_000
        ),
    )(*arrays)


def solution(mesh):
    cells = P("band", "space", None)
    return jax.shard_map(
        functools.partial(per_device, mesh.shape["band"], mesh.shape["space"]),
        mesh=mesh,
        in_specs=(cells, cells, P(), P(), P(), P(), P(), P(), P()),
        out_specs=(cells, cells),
        check_vma=False,
    )
```

time: 57.3 us -> 47.2 us (0.82)
  Pallas kernels: 48.3 us -> 42.9 us
  local copies, waits for them, and re-layouts: 8.09 us -> 3.53 us
    pallas_call x1, Pallas kernels: 48.3 us -> 42.9 us  [per_device(): pl.pallas_call(functools.partial(kernel, bands, spaces), out_shape=(out,...]
    unnamed x16 -> x2, local copies, waits for them, and re-layouts: 8.09 us -> 3.53 us
where the time goes in v2:
time: 47.2 us; the launch traced here: 47 us
  Pallas kernels  42.9 us (91%)
  local copies, waits for them, and re-layouts  3.53 us (7%)
  between operations  0.64 us (1%)
    pallas_call x1, Pallas kernels, per_device(): pl.pallas_call(functools.partial(kernel, bands, spaces), out_shape=(out,...  42.9 us
    unnamed x2, local copies, waits for them, and re-layouts  3.53 us

profile of v2, /device:TPU:1, one launch (start us, length us, event | category | flops | bytes accessed | tf_op | source)
XLA Modules:
  0.0 47.0 jit_solution(1568446700198312840)
XLA Ops:
  0.6 42.9 %shard_map.104 = (f32[1,128,768]{2,1,0:T(8,128)}, f32[1,128,768]{2,1,0:T(8,128)}) custom-call(bf16[1,128,768]{2,1,0:T(8,128)(2,1)} %tok_hbm.1, bf16[1,128,768]{2,1,0:T(8,128)(2,1)} %cot_hbm.1, s32[16,2048]{1,0:T(8,128)} %vis_hbm.1, f32[12]{0:T(128)} %tau_space_hbm.1, f32[12]{0:T(128)} %tau_band_hbm.1, bf16[768,2304]{1,0:T(8,128)(2,1)} %wqs_hbm.1, ...), custom_call_target="tpu_custom_call" | custom-call | flops 3500000000 | bytes 11000000 | tf_op jit(solution)/shard_map/pallas_call | solution.py:551
  43.5 1.8 %copy.13 = f32[1,128,768]{2,1,0:T(8,128)} copy(f32[1,128,768]{2,1,0:T(8,128)} %get-tuple-element.4) | data formatting | bytes 786432
  45.3 1.8 %copy.14 = f32[1,128,768]{2,1,0:T(8,128)} copy(f32[1,128,768]{2,1,0:T(8,128)} %get-tuple-element.5) | data formatting | bytes 786432

commit v3 on v2

--- a/solution.py
+++ b/solution.py
@@ -88,8 +88,8 @@
     wos_hbm,
     wqb_hbm,
     wob_hbm,
-    mixed_hbm,
-    grad_hbm,
+    mixed,
+    grad,
     tok,
     halo,
     cot,
@@ -128,8 +128,6 @@
     sent,
     got,
     got_rim,
-    mixed,
-    grad,
     local_sem,
     near_send,
     near_recv,
@@ -156,8 +154,6 @@
         "wqb": local(wqb_hbm, wqb, 5),
         "tau_space": local(tau_space_hbm, tau_space, 9),
         "tau_band": local(tau_band_hbm, tau_band, 10),
-        "mixed": local(mixed, mixed_hbm.at[0], 11),
-        "grad": local(grad, grad_hbm.at[0], 12),
     }
     for index, block in enumerate((left, space, right)):
         copies["vis%d" % index] = local(
@@ -339,9 +335,9 @@
     for pair in range(PAIRS):
         values[pair, :T, :128] = raw[:, lanes(pair)]
     for pair in range(PAIRS):
-        weight = grown(queries[0, pair], keys[:T, lanes(pair)], mask_own)
-        grown_one[pair, :, :T] = weight
-        partial[pair] = dot(weight, values[pair, :T])
+        grown_one[pair, :, :T] = grown(queries[0, pair], keys[:T, lanes(pair)], mask_own)
+    for pair in range(PAIRS):
+        partial[pair] = dot(grown_one[pair, :, :T], values[pair, :T])
 
     for copy in near[0]:
         copy.wait_recv()
@@ -351,20 +347,21 @@
     raw = dot(normed, wqs[:, 2 * D :]).astype(BF16)
     for pair in range(PAIRS):
         values[pair, T:, :128] = raw[:, lanes(pair)]
-    table = jnp.zeros((T, 128), F32)
-    for pair in range(PAIRS):
-        weight = grown(queries[0, pair], keys[T:, lanes(pair)], mask_rim)
-        grown_one[pair, :, T:] = weight
-        out = partial[pair] + dot(weight, values[pair, T:])
+    for pair in range(PAIRS):
+        grown_one[pair, :, T:] = grown(queries[0, pair], keys[T:, lanes(pair)], mask_rim)
+    for pair in range(PAIRS):
+        out = partial[pair] + dot(grown_one[pair, :, T:], values[pair, T:])
         turned = 1.0 / out[:, 128:]
         inverse[0, pair] = turned
         attended[:, lanes(pair)] = paired(low, out[:, :128] * turned).astype(BF16)
-        table = jnp.where(col == 2 * pair, turned[:T], table)
-        table = jnp.where(col == 2 * pair + 1, turned[T:], table)
-    stats[...] = table
     copies["wos"].wait()
     after[...] = (inputs + dot(attended[...], wos[...])).astype(BF16)
     scatter(1, after[...].astype(F32))
+    table = jnp.zeros((T, 128), F32)
+    for pair in range(PAIRS):
+        table = jnp.where(col == 2 * pair, inverse[0, pair, :T], table)
+        table = jnp.where(col == 2 * pair + 1, inverse[0, pair, T:], table)
+    stats[...] = table
     for index in (1, 2):
         for copy in near[index]:
             copy.start()
@@ -388,23 +385,26 @@
     raw = dot(normed, wqb[:, 2 * D :]).astype(BF16)
     for pair in range(PAIRS):
         values_two[pair, :, :128] = raw[:, lanes(pair)]
-    outs = []
-    for pair in range(PAIRS):
+    everyone = range(PAIRS)
+    weight = [grown(queries[1, p], keys_two[:, lanes(p)], mask_two) for p in everyone]
+    outs, turned = [], []
+    for pair in everyone:
+        out = dot(weight[pair], values_two[pair])
+        turned.append(1.0 / out[:, 128:])
+        outs.append(out[:, :128] * turned[pair])
+    dscore = []
+    for pair in everyone:
+        ups = ups_stack[pair]
+        inside = inner(ups, (-ups.astype(F32) * outs[pair]).astype(BF16), values_two[pair])
+        dscore.append((weight[pair].astype(F32) * (inside * turned[pair])).astype(BF16))
+    for pair in everyone:
         at = lanes(pair)
-        query, key, value, ups = queries[1, pair], keys_two[:, at], values_two[pair], ups_stack[pair]
-        weight = grown(query, key, mask_two)
-        out = dot(weight, value)
-        turned = 1.0 / out[:, 128:]
-        out = out[:, :128] * turned
-        outs.append(paired(low, out))
-        ups_f = ups.astype(F32)
-        dscore = inner(ups, (-ups_f * out).astype(BF16), value) * turned
-        dscore = (weight.astype(F32) * dscore).astype(BF16)
-        grads[:, at] = paired(low, dot(dscore, key)) * scale_band[:, at]
-        grads[:, D + pair * 128 : D + pair * 128 + 128] = dot_tn(dscore, query)
+        grads[:, at] = paired(low, dot(dscore[pair], keys_two[:, at])) * scale_band[:, at]
+        grads[:, D + pair * 128 : D + pair * 128 + 128] = dot_tn(dscore[pair], queries[1, pair])
         wide[:, 2 * D + pair * 128 : 2 * D + pair * 128 + 128] = dot_tn(
-            weight, (ups_f * turned).astype(BF16)
+            weight[pair], (ups_stack[pair].astype(F32) * turned[pair]).astype(BF16)
         ).astype(BF16)
+    outs = [paired(low, out) for out in outs]
     wide[:, :D] = head_back(unit_q[1], fact_q[1], grads[:, :D], ones).astype(BF16)
     wide[:, D : 2 * D] = head_back(unit_k[1], fact_k[1], grads[:, D:], ones).astype(BF16)
     back = dot(wide[...], wqb_t[...])
@@ -430,57 +430,67 @@
 
     grad_after = collect(3)
     grad_att = dot(grad_after.astype(BF16), wos_t[...])
+    def stacked_ups():
+        return [
+            jnp.concatenate(
+                [jnp.where(low, part, 0.0), jnp.where(low, 0.0, part)], axis=0
+            )
+            for part in (grad_att[:, lanes(pair)] for pair in range(PAIRS))
+        ]
+
+    def window_dscore(ups, weight, outs, value, turned):
+        out = jnp.concatenate([outs, outs], axis=0).astype(F32)
+        inside = inner(ups.astype(BF16), (-ups * out).astype(BF16), value)
+        return (weight.astype(F32) * (inside * turned)).astype(BF16)
+
+    ups_all = stacked_ups()
+    dscore = []
+    for pair in range(PAIRS):
+        turned = inverse[0, pair]
+        turned = jnp.concatenate([turned, turned], axis=1)
+        dscore.append(
+            window_dscore(
+                ups_all[pair], grown_one[pair], attended[:, lanes(pair)], values[pair], turned
+            )
+        )
     for pair in range(PAIRS):
         at = lanes(pair)
-        query, value, weight = queries[0, pair], values[pair], grown_one[pair]
-        ups_f = jnp.concatenate(
-            [jnp.where(low, grad_att[:, at], 0.0), jnp.where(low, 0.0, grad_att[:, at])], axis=0
-        )
-        out = attended[:, at].astype(F32)
-        turned = inverse[0, pair]
-        dscore = inner(
-            ups_f.astype(BF16),
-            (-ups_f * jnp.concatenate([out, out], axis=0)).astype(BF16),
-            value,
-        )
-        dscore = dscore * jnp.concatenate([turned, turned], axis=1)
-        dscore = (weight.astype(F32) * dscore).astype(BF16)
-        grads[:, at] = paired(low, dot(dscore, keys[:, at])) * scale_space[:, at]
-        partial[pair, :T, :128] = dot_tn(dscore[:, :T], query)
-        partial[pair, :T, 128:] = dot_tn(weight[:, :T], (ups_f * turned).astype(BF16))
+        grads[:, at] = paired(low, dot(dscore[pair], keys[:, at])) * scale_space[:, at]
+        partial[pair, :T, :128] = dot_tn(dscore[pair][:, :T], queries[0, pair])
+        partial[pair, :T, 128:] = dot_tn(
+            grown_one[pair, :, :T], (ups_all[pair] * inverse[0, pair]).astype(BF16)
+        )
     wide[:, :D] = head_back(unit_q[0], fact_q[0], grads[:, :D], ones).astype(BF16)
     back = dot(wide[:, :D], wqs_t[:D])
-    mixed[...] = after[...].astype(F32) + dot(collect(2).astype(BF16), wob[...])
-    copies["mixed"].start()
+    mixed[0] = after[...].astype(F32) + dot(collect(2).astype(BF16), wob[...])
 
     for sender in range(bands):
         far_arrival(sender).wait_recv()
     grad_att = dot(unpacked(got_rim[...]).astype(BF16), wos_t[...])
-    for pair in range(PAIRS):
-        at = lanes(pair)
-        query, weight, turned = queries[2, pair], grown_rim[pair], inverse_rim[pair]
-        ups_f = jnp.concatenate(
-            [jnp.where(low, grad_att[:, at], 0.0), jnp.where(low, 0.0, grad_att[:, at])], axis=0
-        )
-        out = attended_rim[:, at].astype(F32)
-        dscore = inner(
-            ups_f.astype(BF16),
-            (-ups_f * jnp.concatenate([out, out], axis=0)).astype(BF16),
+    ups_all = stacked_ups()
+    dscore = [
+        window_dscore(
+            ups_all[pair],
+            grown_rim[pair],
+            attended_rim[:, lanes(pair)],
             values[pair, :T],
-        )
-        dscore = (weight.astype(F32) * (dscore * turned)).astype(BF16)
+            inverse_rim[pair],
+        )
+        for pair in range(PAIRS)
+    ]
+    for pair in range(PAIRS):
         grads[:, D + pair * 128 : D + pair * 128 + 128] = partial[pair, :T, :128] + dot_tn(
-            dscore, query
+            dscore[pair], queries[2, pair]
         )
         wide[:, 2 * D + pair * 128 : 2 * D + pair * 128 + 128] = (
-            partial[pair, :T, 128:] + dot_tn(weight, (ups_f * turned).astype(BF16))
+            partial[pair, :T, 128:]
+            + dot_tn(grown_rim[pair], (ups_all[pair] * inverse_rim[pair]).astype(BF16))
         ).astype(BF16)
     wide[:, D : 2 * D] = head_back(unit_k[0], fact_k[0], grads[:, D:], ones).astype(BF16)
     back = back + dot(wide[:, D:], wqs_t[D:])
     inputs = tok[...].astype(F32)
     fact_one = row_factor(inputs)
-    grad[...] = grad_after + row_back(inputs * fact_one, fact_one, back)
-    copies["grad"].start()
+    grad[0] = grad_after + row_back(inputs * fact_one, fact_one, back)
 
     for index in range(3):
         for copy in near[index]:
@@ -490,11 +500,27 @@
             exchange(phase, step).wait_send()
     for step in range(bands):
         far(step).wait_send()
-    copies["mixed"].wait()
-    copies["grad"].wait()
+
+
+def deliver(mixed, grad, mixed_hbm, grad_hbm, sem):
+    copies = [
+        pltpu.make_async_copy(
+            source.at[0, pl.ds(part * 32, 32)],
+            target.at[0, pl.ds(part * 32, 32)],
+            sem.at[which, part],
+        )
+        for part in range(4)
+        for which, (source, target) in enumerate(((mixed, mixed_hbm), (grad, grad_hbm)))
+    ]
+    for copy in copies:
+        copy.start()
+    for copy in copies:
+        copy.wait()
 
 
 def per_device(bands, spaces, *arrays):
+    kept = pltpu.VMEM((1, T, D), F32)
+    vmem = pl.BlockSpec(memory_space=pltpu.VMEM)
     hbm = pl.BlockSpec(memory_space=pltpu.HBM)
     out = jax.ShapeDtypeStruct((1, T, D), F32)
     count = T // bands
@@ -538,9 +564,7 @@
         pltpu.VMEM((4, bands, 2 * count, HALF), BF16),
         pltpu.VMEM((4, bands, 2 * count, HALF), BF16),
         pltpu.VMEM((bands, 2 * count, HALF), BF16),
-        pltpu.VMEM((T, D), F32),
-        pltpu.VMEM((T, D), F32),
-        dma((13,)),
+        dma((11,)),
         dma((3, 2)),
         dma((3, 2)),
         dma((4, bands)),
@@ -548,19 +572,26 @@
         dma((bands,)),
         dma((bands,)),
     ]
-    return pl.pallas_call(
+    made = pl.pallas_call(
         functools.partial(kernel, bands, spaces),
-        out_shape=(out, out),
+        out_shape=(kept, kept),
         in_specs=[hbm] * 9,
-        out_specs=(hbm, hbm),
+        out_specs=(vmem, vmem),
         scratch_shapes=scratch,
         compiler_params=pltpu.CompilerParams(
-            collective_id=0, has_side_effects=True, vmem_limit_bytes=64 * 1024 * 1024 - 65536
+            collective_id=0, has_side_effects=True, vmem_limit_bytes=63 * 1024 * 1024
         ),
         cost_estimate=pl.CostEstimate(
             flops=3_500_000_000, bytes_accessed=11_000_000, transcendentals=600_000
         ),
     )(*arrays)
+    return pl.pallas_call(
+        deliver,
+        out_shape=(out, out),
+        in_specs=[vmem] * 2,
+        out_specs=(hbm, hbm),
+        scratch_shapes=[dma((2, 4))],
+    )(*[pltpu.with_memory_space_constraint(part, pltpu.VMEM) for part in made])
 
 
 def solution(mesh):

time: 47.2 us -> 41.2 us (0.87)
  local copies, waits for them, and re-layouts: 3.53 us -> 0 us
  Pallas kernels: 42.9 us -> 40.5 us
    unnamed x2 -> x0, local copies, waits for them, and re-layouts: 3.53 us -> none
    pallas_call x1 -> x2, Pallas kernels: 42.9 us -> 40.5 us  [the longest x1 39.5 us: per_device(): pl.pallas_call(functools.partial(kernel, bands, spaces), out_shape=(kept,...]
where the time goes in v3:
time: 41.2 us; the launch traced here: 41.1 us
  Pallas kernels  40.5 us (98%)
  between operations  0.64 us (2%)
    pallas_call x1, Pallas kernels, per_device(): pl.pallas_call(functools.partial(kernel, bands, spaces), out_shape=(kept,...  39.5 us
    pallas_call x1, Pallas kernels, per_device(): pl.pallas_call(deliver, out_shape=(out, out), in_specs=[vmem] * 2, out_sp...  0.94 us

profile of v3, /device:TPU:1, one launch (start us, length us, event | category | flops | bytes accessed | tf_op | source)
XLA Modules:
  0.0 41.1 jit_solution(8741205116644813815)
XLA Ops:
  0.6 39.5 %shard_map.104 = (f32[1,128,768]{2,1,0:T(8,128)S(1)}, f32[1,128,768]{2,1,0:T(8,128)S(1)}) custom-call(bf16[1,128,768]{2,1,0:T(8,128)(2,1)} %tok_hbm.1, bf16[1,128,768]{2,1,0:T(8,128)(2,1)} %cot_hbm.1, s32[16,2048]{1,0:T(8,128)} %vis_hbm.1, f32[12]{0:T(128)} %tau_space_hbm.1, f32[12]{0:T(128)} %tau_band_hbm.1, bf16[768,2304]{1,0:T(8,128)(2,1)} %wqs_hbm.1, ...), custom_call_target="tpu_custom_call" | custom-call | flops 3500000000 | bytes 11000000 | tf_op jit(solution)/shard_map/pallas_call | solution.py:575
  40.2 0.9 %shard_map.105 = (f32[1,128,768]{2,1,0:T(8,128)}, f32[1,128,768]{2,1,0:T(8,128)}) custom-call(f32[1,128,768]{2,1,0:T(8,128)S(1)} %get-tuple-element.4.mixed, f32[1,128,768]{2,1,0:T(8,128)S(1)} %get-tuple-element.5.grad), custom_call_target="tpu_custom_call" | custom-call | tf_op jit(solution)/shard_map/pallas_call | solution.py:588

commit v4 on v3

--- a/solution.py
+++ b/solution.py
@@ -263,9 +263,6 @@
         values[pair, :, 128:] = jnp.ones((2 * T, 128), BF16)
         values_two[pair, :, 128:] = jnp.ones((T, 128), BF16)
 
-    copies["cot"].wait()
-    scatter(0, cot[...].astype(F32))
-
     for index in range(3):
         copies["vis%d" % index].wait()
     group = lax.broadcasted_iota(jnp.int32, (bands, 128), 0)
@@ -339,6 +336,9 @@
     for pair in range(PAIRS):
         partial[pair] = dot(grown_one[pair, :, :T], values[pair, :T])
 
+    copies["cot"].wait()
+    scatter(0, cot[...].astype(F32))
+
     for copy in near[0]:
         copy.wait_recv()
     rim = halo[...].astype(F32)
@@ -362,9 +362,6 @@
         table = jnp.where(col == 2 * pair, inverse[0, pair, :T], table)
         table = jnp.where(col == 2 * pair + 1, inverse[0, pair, T:], table)
     stats[...] = table
-    for index in (1, 2):
-        for copy in near[index]:
-            copy.start()
 
     upstream = collect(0)
     copies["wob"].wait()
@@ -377,6 +374,9 @@
         wqb_t[at : at + 256] = wqb[:, at : at + 256].T
 
     rows = collect(1)
+    for index in (1, 2):
+        for copy in near[index]:
+            copy.start()
     fact_two = row_factor(rows)
     unit_two = rows * fact_two
     normed = unit_two.astype(BF16)
@@ -392,6 +392,7 @@
         out = dot(weight[pair], values_two[pair])
         turned.append(1.0 / out[:, 128:])
         outs.append(out[:, :128] * turned[pair])
+    scatter(2, jnp.concatenate([paired(low, out) for out in outs], axis=1))
     dscore = []
     for pair in everyone:
         ups = ups_stack[pair]
@@ -404,14 +405,12 @@
         wide[:, 2 * D + pair * 128 : 2 * D + pair * 128 + 128] = dot_tn(
             weight[pair], (ups_stack[pair].astype(F32) * turned[pair]).astype(BF16)
         ).astype(BF16)
-    outs = [paired(low, out) for out in outs]
     wide[:, :D] = head_back(unit_q[1], fact_q[1], grads[:, :D], ones).astype(BF16)
     wide[:, D : 2 * D] = head_back(unit_k[1], fact_k[1], grads[:, D:], ones).astype(BF16)
     back = dot(wide[...], wqb_t[...])
     scatter(3, upstream + row_back(unit_two, fact_two, back))
     for step in range(bands):
         far(step).start()
-    scatter(2, jnp.concatenate(outs, axis=1))
 
     for at in range(0, 3 * D, 256):
         wqs_t[at : at + 256] = wqs[:, at : at + 256].T

time: 41.2 us -> 41.3 us (level)
  no operation moved by 1% of the time
where the time goes in v4:
time: 41.3 us; the launch traced here: 41.2 us
  Pallas kernels  40.6 us (98%)
  between operations  0.64 us (2%)
    pallas_call x1, Pallas kernels, per_device(): pl.pallas_call(functools.partial(kernel, bands, spaces), out_shape=(kept,...  39.7 us
    pallas_call x1, Pallas kernels, per_device(): pl.pallas_call(deliver, out_shape=(out, out), in_specs=[vmem] * 2, out_sp...  0.94 us

profile of v4, /device:TPU:1, one launch (start us, length us, event | category | flops | bytes accessed | tf_op | source)
XLA Modules:
  0.0 41.2 jit_solution(15030464207340773159)
XLA Ops:
  0.6 39.7 %shard_map.104 = (f32[1,128,768]{2,1,0:T(8,128)S(1)}, f32[1,128,768]{2,1,0:T(8,128)S(1)}) custom-call(bf16[1,128,768]{2,1,0:T(8,128)(2,1)} %tok_hbm.1, bf16[1,128,768]{2,1,0:T(8,128)(2,1)} %cot_hbm.1, s32[16,2048]{1,0:T(8,128)} %vis_hbm.1, f32[12]{0:T(128)} %tau_space_hbm.1, f32[12]{0:T(128)} %tau_band_hbm.1, bf16[768,2304]{1,0:T(8,128)(2,1)} %wqs_hbm.1, ...), custom_call_target="tpu_custom_call" | custom-call | flops 3500000000 | bytes 11000000 | tf_op jit(solution)/shard_map/pallas_call | solution.py:574
  40.3 0.9 %shard_map.105 = (f32[1,128,768]{2,1,0:T(8,128)}, f32[1,128,768]{2,1,0:T(8,128)}) custom-call(f32[1,128,768]{2,1,0:T(8,128)S(1)} %get-tuple-element.4.mixed, f32[1,128,768]{2,1,0:T(8,128)S(1)} %get-tuple-element.5.grad), custom_call_target="tpu_custom_call" | custom-call | tf_op jit(solution)/shard_map/pallas_call | solution.py:587

commit v5 on v4

--- a/solution.py
+++ b/solution.py
@@ -139,6 +139,7 @@
     band = lax.axis_index("band")
     space = lax.axis_index("space")
     count = T // bands
+    chunk = lax.div(band, 2) + (bands // 2) * lax.rem(band, 2)
     right = lax.rem(space + 1, spaces)
     left = lax.rem(space + spaces - 1, spaces)
 
@@ -199,12 +200,23 @@
 
     def exchange(phase, step):
         other = lax.rem(band + step, bands)
+        away = lax.div(other, 2) + (bands // 2) * lax.rem(other, 2)
         return pltpu.make_async_remote_copy(
-            src_ref=sent.at[phase, other],
-            dst_ref=got.at[phase, band],
-            send_sem=all_send.at[phase, step],
-            recv_sem=all_recv.at[phase, step],
+            src_ref=sent.at[phase, away if phase < 2 else other],
+            dst_ref=got.at[phase, band if phase < 2 else chunk],
+            send_sem=all_send.at[phase],
+            recv_sem=all_recv.at[phase],
             device_id=(other, space),
+            device_id_type=MESH,
+        )
+
+    def whole(phase):
+        return pltpu.make_async_remote_copy(
+            src_ref=sent.at[phase, pl.ds(0, bands - 1)],
+            dst_ref=got.at[phase, pl.ds(0, bands - 1)],
+            send_sem=all_send.at[phase],
+            recv_sem=all_recv.at[phase],
+            device_id=(lax.rem(band + 1, bands), space),
             device_id_type=MESH,
         )
 
@@ -216,7 +228,10 @@
         sent[phase] = jnp.concatenate(pieces, axis=1).astype(BF16)
         for step in range(1, bands):
             exchange(phase, step).start()
-        got[phase, band] = sent[phase, band]
+        if phase < 2:
+            got[phase, band] = sent[phase, chunk]
+        else:
+            got[phase, chunk] = sent[phase, band]
 
     def unpacked(slots):
         rows = slots.astype(F32)
@@ -225,32 +240,30 @@
         )
 
     def collect(phase):
-        for step in range(1, bands):
-            exchange(phase, step).wait_recv()
+        whole(phase).wait_recv()
         return unpacked(got[phase])
 
-    toward = lax.rem(space + spaces - 1 + 2 * lax.div(band, bands // 2), spaces)
+    toward = lax.rem(space + spaces - 1 + 2 * lax.rem(band, 2), spaces)
 
     def far(step):
         other = lax.rem(band + step, bands)
         return pltpu.make_async_remote_copy(
             src_ref=sent.at[3, other],
-            dst_ref=got_rim.at[band],
-            send_sem=far_send.at[step],
-            recv_sem=far_recv.at[band],
+            dst_ref=got_rim.at[chunk],
+            send_sem=far_send,
+            recv_sem=far_recv,
             device_id=(other, toward),
             device_id_type=MESH,
         )
 
-    def far_arrival(sender):
-        return pltpu.make_async_remote_copy(
-            src_ref=sent.at[3, sender],
-            dst_ref=got_rim.at[sender],
-            send_sem=far_send.at[sender],
-            recv_sem=far_recv.at[sender],
-            device_id=(band, toward),
-            device_id_type=MESH,
-        )
+    far_whole = pltpu.make_async_remote_copy(
+        src_ref=sent.at[3],
+        dst_ref=got_rim,
+        send_sem=far_send,
+        recv_sem=far_recv,
+        device_id=(band, toward),
+        device_id_type=MESH,
+    )
 
     low = lax.broadcasted_iota(jnp.int32, (T, 128), 1) < HEAD_DIM
     ones = jnp.where(
@@ -285,7 +298,7 @@
     mask_own = flag(within(row - col) & (own_seen | (row == col)))
     mask_rim = flag(within(jnp.where(col < RADIUS, col + T, col - T) - row) & rim_seen)
     mask_back = flag(within(jnp.where(row < RADIUS, row + T, row - T) - col) & own_seen)
-    pick = flag(row == band * count + lax.rem(col, count))
+    pick = flag(row == chunk * count + lax.rem(col, count))
     spread = dot(vis[1].astype(F32), pick)
     seen = jnp.sum(
         jnp.where(group == lax.div(lane, count), spread, 0.0), axis=0, keepdims=True
@@ -463,8 +476,12 @@
     back = dot(wide[:, :D], wqs_t[:D])
     mixed[0] = after[...].astype(F32) + dot(collect(2).astype(BF16), wob[...])
 
-    for sender in range(bands):
-        far_arrival(sender).wait_recv()
+    for index in range(3):
+        for copy in near[index]:
+            copy.wait_send()
+    for phase in range(4):
+        whole(phase).wait_send()
+    far_whole.wait_recv()
     grad_att = dot(unpacked(got_rim[...]).astype(BF16), wos_t[...])
     ups_all = stacked_ups()
     dscore = [
@@ -491,14 +508,7 @@
     fact_one = row_factor(inputs)
     grad[0] = grad_after + row_back(inputs * fact_one, fact_one, back)
 
-    for index in range(3):
-        for copy in near[index]:
-            copy.wait_send()
-    for phase in range(4):
-        for step in range(1, bands):
-            exchange(phase, step).wait_send()
-    for step in range(bands):
-        far(step).wait_send()
+    far_whole.wait_send()
 
 
 def deliver(mixed, grad, mixed_hbm, grad_hbm, sem):
@@ -566,10 +576,10 @@
         dma((11,)),
         dma((3, 2)),
         dma((3, 2)),
-        dma((4, bands)),
-        dma((4, bands)),
-        dma((bands,)),
-        dma((bands,)),
+        dma((4,)),
+        dma((4,)),
+        dma,
+        dma,
     ]
     made = pl.pallas_call(
         functools.partial(kernel, bands, spaces),

time: 41.3 us -> 39.4 us (0.954)
  Pallas kernels: 40.6 us -> 38.7 us
    pallas_call x1, Pallas kernels: 39.7 us -> 37.8 us  [per_device(): pl.pallas_call(functools.partial(kernel, bands, spaces), out_shape=(kept,...]
where the time goes in v5:
time: 39.4 us; the launch traced here: 39.3 us
  Pallas kernels  38.7 us (98%)
  between operations  0.64 us (2%)
    pallas_call x1, Pallas kernels, per_device(): pl.pallas_call(functools.partial(kernel, bands, spaces), out_shape=(kept,...  37.8 us
    pallas_call x1, Pallas kernels, per_device(): pl.pallas_call(deliver, out_shape=(out, out), in_specs=[vmem] * 2, out_sp...  0.94 us

profile of v5, /device:TPU:1, one launch (start us, length us, event | category | flops | bytes accessed | tf_op | source)
XLA Modules:
  0.0 39.3 jit_solution(6765242862400764639)
XLA Ops:
  0.6 37.8 %shard_map.104 = (f32[1,128,768]{2,1,0:T(8,128)S(1)}, f32[1,128,768]{2,1,0:T(8,128)S(1)}) custom-call(bf16[1,128,768]{2,1,0:T(8,128)(2,1)} %tok_hbm.1, bf16[1,128,768]{2,1,0:T(8,128)(2,1)} %cot_hbm.1, s32[16,2048]{1,0:T(8,128)} %vis_hbm.1, f32[12]{0:T(128)} %tau_space_hbm.1, f32[12]{0:T(128)} %tau_band_hbm.1, bf16[768,2304]{1,0:T(8,128)(2,1)} %wqs_hbm.1, ...), custom_call_target="tpu_custom_call" | custom-call | flops 3500000000 | bytes 11000000 | tf_op jit(solution)/shard_map/pallas_call | solution.py:584
  38.4 0.9 %shard_map.105 = (f32[1,128,768]{2,1,0:T(8,128)}, f32[1,128,768]{2,1,0:T(8,128)}) custom-call(f32[1,128,768]{2,1,0:T(8,128)S(1)} %get-tuple-element.4.mixed, f32[1,128,768]{2,1,0:T(8,128)S(1)} %get-tuple-element.5.grad), custom_call_target="tpu_custom_call" | custom-call | tf_op jit(solution)/shard_map/pallas_call | solution.py:597

commit v6 on v5

--- a/solution.py
+++ b/solution.py
@@ -128,6 +128,10 @@
     sent,
     got,
     got_rim,
+    sent_four,
+    got_four,
+    sent_two,
+    got_two,
     local_sem,
     near_send,
     near_recv,
@@ -198,12 +202,15 @@
     for copy in near[0]:
         copy.start()
 
+    outbox = [sent.at[0], sent.at[1], sent.at[2], sent_four, sent_two]
+    inbox = [got.at[0], got.at[1], got.at[2], got_four, got_two]
+
     def exchange(phase, step):
         other = lax.rem(band + step, bands)
         away = lax.div(other, 2) + (bands // 2) * lax.rem(other, 2)
         return pltpu.make_async_remote_copy(
-            src_ref=sent.at[phase, away if phase < 2 else other],
-            dst_ref=got.at[phase, band if phase < 2 else chunk],
+            src_ref=outbox[phase].at[away if phase < 2 else other],
+            dst_ref=inbox[phase].at[band if phase < 2 else chunk],
             send_sem=all_send.at[phase],
             recv_sem=all_recv.at[phase],
             device_id=(other, space),
@@ -212,8 +219,8 @@
 
     def whole(phase):
         return pltpu.make_async_remote_copy(
-            src_ref=sent.at[phase, pl.ds(0, bands - 1)],
-            dst_ref=got.at[phase, pl.ds(0, bands - 1)],
+            src_ref=outbox[phase].at[pl.ds(0, bands - 1)],
+            dst_ref=inbox[phase].at[pl.ds(0, bands - 1)],
             send_sem=all_send.at[phase],
             recv_sem=all_recv.at[phase],
             device_id=(lax.rem(band + 1, bands), space),
@@ -221,34 +228,36 @@
         )
 
     def scatter(phase, rows):
+        half = rows.shape[1] // 2
         pieces = [
-            rows[:, :HALF].reshape(bands, count, HALF),
-            rows[:, HALF:].reshape(bands, count, HALF),
+            rows[:, :half].reshape(bands, count, half),
+            rows[:, half:].reshape(bands, count, half),
         ]
-        sent[phase] = jnp.concatenate(pieces, axis=1).astype(BF16)
+        outbox[phase][...] = jnp.concatenate(pieces, axis=1).astype(BF16)
         for step in range(1, bands):
             exchange(phase, step).start()
         if phase < 2:
-            got[phase, band] = sent[phase, chunk]
+            inbox[phase][band] = outbox[phase][chunk]
         else:
-            got[phase, chunk] = sent[phase, band]
+            inbox[phase][chunk] = outbox[phase][band]
 
     def unpacked(slots):
         rows = slots.astype(F32)
+        half = rows.shape[2]
         return jnp.concatenate(
-            [rows[:, :count].reshape(T, HALF), rows[:, count:].reshape(T, HALF)], axis=1
+            [rows[:, :count].reshape(T, half), rows[:, count:].reshape(T, half)], axis=1
         )
 
     def collect(phase):
         whole(phase).wait_recv()
-        return unpacked(got[phase])
+        return unpacked(inbox[phase][...])
 
     toward = lax.rem(space + spaces - 1 + 2 * lax.rem(band, 2), spaces)
 
     def far(step):
         other = lax.rem(band + step, bands)
         return pltpu.make_async_remote_copy(
-            src_ref=sent.at[3, other],
+            src_ref=sent.at[2, other],
             dst_ref=got_rim.at[chunk],
             send_sem=far_send,
             recv_sem=far_recv,
@@ -257,7 +266,7 @@
         )
 
     far_whole = pltpu.make_async_remote_copy(
-        src_ref=sent.at[3],
+        src_ref=sent.at[2],
         dst_ref=got_rim,
         send_sem=far_send,
         recv_sem=far_recv,
@@ -386,10 +395,10 @@
     for at in range(0, 3 * D, 256):
         wqb_t[at : at + 256] = wqb[:, at : at + 256].T
 
-    rows = collect(1)
     for index in (1, 2):
         for copy in near[index]:
             copy.start()
+    rows = collect(1)
     fact_two = row_factor(rows)
     unit_two = rows * fact_two
     normed = unit_two.astype(BF16)
@@ -405,7 +414,7 @@
         out = dot(weight[pair], values_two[pair])
         turned.append(1.0 / out[:, 128:])
         outs.append(out[:, :128] * turned[pair])
-    scatter(2, jnp.concatenate([paired(low, out) for out in outs], axis=1))
+    scatter(3, jnp.concatenate([paired(low, out) for out in outs[:4]], axis=1))
     dscore = []
     for pair in everyone:
         ups = ups_stack[pair]
@@ -421,26 +430,19 @@
     wide[:, :D] = head_back(unit_q[1], fact_q[1], grads[:, :D], ones).astype(BF16)
     wide[:, D : 2 * D] = head_back(unit_k[1], fact_k[1], grads[:, D:], ones).astype(BF16)
     back = dot(wide[...], wqb_t[...])
-    scatter(3, upstream + row_back(unit_two, fact_two, back))
+    scatter(2, upstream + row_back(unit_two, fact_two, back))
     for step in range(bands):
         far(step).start()
+    scatter(4, jnp.concatenate([paired(low, out) for out in outs[4:]], axis=1))
 
     for at in range(0, 3 * D, 256):
         wqs_t[at : at + 256] = wqs[:, at : at + 256].T
     for at in range(0, D, 256):
         wos_t[at : at + 256] = wos[:, at : at + 256].T
-    for index in (1, 2):
-        for copy in near[index]:
-            copy.wait_recv()
     for pair in range(PAIRS):
         grown_rim[pair] = grown(queries[2, pair], keys[:T, lanes(pair)], mask_back)
-        for part in range(2):
-            head = 2 * pair + part
-            inverse_rim[pair, part * T : part * T + T] = jnp.broadcast_to(
-                stats_rim[:, head : head + 1], (T, 128)
-            )
-
-    grad_after = collect(3)
+
+    grad_after = collect(2)
     grad_att = dot(grad_after.astype(BF16), wos_t[...])
     def stacked_ups():
         return [
@@ -474,7 +476,16 @@
         )
     wide[:, :D] = head_back(unit_q[0], fact_q[0], grads[:, :D], ones).astype(BF16)
     back = dot(wide[:, :D], wqs_t[:D])
-    mixed[0] = after[...].astype(F32) + dot(collect(2).astype(BF16), wob[...])
+    mixed[0] = after[...].astype(F32) + dot(collect(3).astype(BF16), wob[:512])
+    for index in (1, 2):
+        for copy in near[index]:
+            copy.wait_recv()
+    for pair in range(PAIRS):
+        for part in range(2):
+            head = 2 * pair + part
+            inverse_rim[pair, part * T : part * T + T] = jnp.broadcast_to(
+                stats_rim[:, head : head + 1], (T, 128)
+            )
 
     for index in range(3):
         for copy in near[index]:
@@ -506,9 +517,11 @@
     back = back + dot(wide[:, D:], wqs_t[D:])
     inputs = tok[...].astype(F32)
     fact_one = row_factor(inputs)
+    mixed[0] += dot(collect(4).astype(BF16), wob[512:])
     grad[0] = grad_after + row_back(inputs * fact_one, fact_one, back)
 
     far_whole.wait_send()
+    whole(4).wait_send()
 
 
 def deliver(mixed, grad, mixed_hbm, grad_hbm, sem):
@@ -570,14 +583,18 @@
         pltpu.VMEM((T, 128), F32),
         pltpu.VMEM((T, 128), F32),
         pltpu.VMEM((T, 2 * D), F32),
-        pltpu.VMEM((4, bands, 2 * count, HALF), BF16),
-        pltpu.VMEM((4, bands, 2 * count, HALF), BF16),
+        pltpu.VMEM((3, bands, 2 * count, HALF), BF16),
+        pltpu.VMEM((3, bands, 2 * count, HALF), BF16),
         pltpu.VMEM((bands, 2 * count, HALF), BF16),
+        pltpu.VMEM((bands, 2 * count, 256), BF16),
+        pltpu.VMEM((bands, 2 * count, 256), BF16),
+        pltpu.VMEM((bands, 2 * count, 128), BF16),
+        pltpu.VMEM((bands, 2 * count, 128), BF16),
         dma((11,)),
         dma((3, 2)),
         dma((3, 2)),
-        dma((4,)),
-        dma((4,)),
+        dma((5,)),
+        dma((5,)),
         dma,
         dma,
     ]

time: 39.4 us -> 39.3 us (level)
  no operation moved by 1% of the time
where the time goes in v6:
time: 39.3 us; the launch traced here: 39.2 us
  Pallas kernels  38.6 us (98%)
  between operations  0.64 us (2%)
    pallas_call x1, Pallas kernels, per_device(): pl.pallas_call(functools.partial(kernel, bands, spaces), out_shape=(kept,...  37.6 us
    pallas_call x1, Pallas kernels, per_device(): pl.pallas_call(deliver, out_shape=(out, out), in_specs=[vmem] * 2, out_sp...  0.94 us

profile of v6, /device:TPU:1, one launch (start us, length us, event | category | flops | bytes accessed | tf_op | source)
XLA Modules:
  0.0 39.2 jit_solution(10844891246914268435)
XLA Ops:
  0.6 37.6 %shard_map.104 = (f32[1,128,768]{2,1,0:T(8,128)S(1)}, f32[1,128,768]{2,1,0:T(8,128)S(1)}) custom-call(bf16[1,128,768]{2,1,0:T(8,128)(2,1)} %tok_hbm.1, bf16[1,128,768]{2,1,0:T(8,128)(2,1)} %cot_hbm.1, s32[16,2048]{1,0:T(8,128)} %vis_hbm.1, f32[12]{0:T(128)} %tau_space_hbm.1, f32[12]{0:T(128)} %tau_band_hbm.1, bf16[768,2304]{1,0:T(8,128)(2,1)} %wqs_hbm.1, ...), custom_call_target="tpu_custom_call" | custom-call | flops 3500000000 | bytes 11000000 | tf_op jit(solution)/shard_map/pallas_call | solution.py:601
  38.3 0.9 %shard_map.105 = (f32[1,128,768]{2,1,0:T(8,128)}, f32[1,128,768]{2,1,0:T(8,128)}) custom-call(f32[1,128,768]{2,1,0:T(8,128)S(1)} %get-tuple-element.4.mixed, f32[1,128,768]{2,1,0:T(8,128)S(1)} %get-tuple-element.5.grad), custom_call_target="tpu_custom_call" | custom-call | tf_op jit(solution)/shard_map/pallas_call | solution.py:614

commit v7 on v6

--- a/solution.py
+++ b/solution.py
@@ -128,6 +128,7 @@
     sent,
     got,
     got_rim,
+    sent_far,
     sent_four,
     got_four,
     sent_two,
@@ -195,15 +196,18 @@
         ]
 
     near = [
-        neighbours(tok_hbm.at[0], halo, 0),
+        neighbours(tok, halo, 0),
         neighbours(attended, attended_rim, 1),
         neighbours(stats, stats_rim, 2),
     ]
+    copies["tok"].wait()
     for copy in near[0]:
         copy.start()
 
     outbox = [sent.at[0], sent.at[1], sent.at[2], sent_four, sent_two]
     inbox = [got.at[0], got.at[1], got.at[2], got_four, got_two]
+
+    farthest_first = sorted(range(1, bands), key=lambda step: abs(step - bands // 2))
 
     def exchange(phase, step):
         other = lax.rem(band + step, bands)
@@ -227,14 +231,17 @@
             device_id_type=MESH,
         )
 
-    def scatter(phase, rows):
+    def packed(rows):
         half = rows.shape[1] // 2
         pieces = [
             rows[:, :half].reshape(bands, count, half),
             rows[:, half:].reshape(bands, count, half),
         ]
-        outbox[phase][...] = jnp.concatenate(pieces, axis=1).astype(BF16)
-        for step in range(1, bands):
+        return jnp.concatenate(pieces, axis=1).astype(BF16)
+
+    def scatter(phase, rows):
+        outbox[phase][...] = packed(rows)
+        for step in farthest_first:
             exchange(phase, step).start()
         if phase < 2:
             inbox[phase][band] = outbox[phase][chunk]
@@ -257,7 +264,7 @@
     def far(step):
         other = lax.rem(band + step, bands)
         return pltpu.make_async_remote_copy(
-            src_ref=sent.at[2, other],
+            src_ref=sent_far.at[other],
             dst_ref=got_rim.at[chunk],
             send_sem=far_send,
             recv_sem=far_recv,
@@ -266,7 +273,7 @@
         )
 
     far_whole = pltpu.make_async_remote_copy(
-        src_ref=sent.at[2],
+        src_ref=sent_far,
         dst_ref=got_rim,
         send_sem=far_send,
         recv_sem=far_recv,
@@ -342,7 +349,6 @@
             which[1][slot] = factor
         return unit
 
-    copies["tok"].wait()
     inputs = tok[...].astype(F32)
     normed = (inputs * row_factor(inputs)).astype(BF16)
     copies["wqs"].wait()
@@ -395,6 +401,8 @@
     for at in range(0, 3 * D, 256):
         wqb_t[at : at + 256] = wqb[:, at : at + 256].T
 
+    for at in range(0, D, 256):
+        wos_t[at : at + 256] = wos[:, at : at + 256].T
     for index in (1, 2):
         for copy in near[index]:
             copy.start()
@@ -430,15 +438,15 @@
     wide[:, :D] = head_back(unit_q[1], fact_q[1], grads[:, :D], ones).astype(BF16)
     wide[:, D : 2 * D] = head_back(unit_k[1], fact_k[1], grads[:, D:], ones).astype(BF16)
     back = dot(wide[...], wqb_t[...])
-    scatter(2, upstream + row_back(unit_two, fact_two, back))
-    for step in range(bands):
+    grad_after = upstream + row_back(unit_two, fact_two, back)
+    scatter(2, grad_after)
+    sent_far[...] = packed(dot(grad_after.astype(BF16), wos_t[...]))
+    for step in farthest_first + [0]:
         far(step).start()
     scatter(4, jnp.concatenate([paired(low, out) for out in outs[4:]], axis=1))
 
     for at in range(0, 3 * D, 256):
         wqs_t[at : at + 256] = wqs[:, at : at + 256].T
-    for at in range(0, D, 256):
-        wos_t[at : at + 256] = wos[:, at : at + 256].T
     for pair in range(PAIRS):
         grown_rim[pair] = grown(queries[2, pair], keys[:T, lanes(pair)], mask_back)
 
@@ -493,7 +501,7 @@
     for phase in range(4):
         whole(phase).wait_send()
     far_whole.wait_recv()
-    grad_att = dot(unpacked(got_rim[...]).astype(BF16), wos_t[...])
+    grad_att = unpacked(got_rim[...])
     ups_all = stacked_ups()
     dscore = [
         window_dscore(
@@ -586,6 +594,7 @@
         pltpu.VMEM((3, bands, 2 * count, HALF), BF16),
         pltpu.VMEM((3, bands, 2 * count, HALF), BF16),
         pltpu.VMEM((bands, 2 * count, HALF), BF16),
+        pltpu.VMEM((bands, 2 * count, HALF), BF16),
         pltpu.VMEM((bands, 2 * count, 256), BF16),
         pltpu.VMEM((bands, 2 * count, 256), BF16),
         pltpu.VMEM((bands, 2 * count, 128), BF16),

time: 39.3 us -> 39.7 us (1.010)
  no operation moved by 1% of the time
where the time goes in v7:
time: 39.7 us; the launch traced here: 39.6 us
  Pallas kernels  38.9 us (98%)
  between operations  0.64 us (2%)
    pallas_call x1, Pallas kernels, per_device(): pl.pallas_call(functools.partial(kernel, bands, spaces), out_shape=(kept,...  38 us
    pallas_call x1, Pallas kernels, per_device(): pl.pallas_call(deliver, out_shape=(out, out), in_specs=[vmem] * 2, out_sp...  0.94 us

profile of v7, /device:TPU:1, one launch (start us, length us, event | category | flops | bytes accessed | tf_op | source)
XLA Modules:
  0.0 39.6 jit_solution(16680733092118096589)
XLA Ops:
  0.6 38.0 %shard_map.104 = (f32[1,128,768]{2,1,0:T(8,128)S(1)}, f32[1,128,768]{2,1,0:T(8,128)S(1)}) custom-call(bf16[1,128,768]{2,1,0:T(8,128)(2,1)} %tok_hbm.1, bf16[1,128,768]{2,1,0:T(8,128)(2,1)} %cot_hbm.1, s32[16,2048]{1,0:T(8,128)} %vis_hbm.1, f32[12]{0:T(128)} %tau_space_hbm.1, f32[12]{0:T(128)} %tau_band_hbm.1, bf16[768,2304]{1,0:T(8,128)(2,1)} %wqs_hbm.1, ...), custom_call_target="tpu_custom_call" | custom-call | flops 3500000000 | bytes 11000000 | tf_op jit(solution)/shard_map/pallas_call | solution.py:610
  38.6 0.9 %shard_map.105 = (f32[1,128,768]{2,1,0:T(8,128)}, f32[1,128,768]{2,1,0:T(8,128)}) custom-call(f32[1,128,768]{2,1,0:T(8,128)S(1)} %get-tuple-element.4.mixed, f32[1,128,768]{2,1,0:T(8,128)S(1)} %get-tuple-element.5.grad), custom_call_target="tpu_custom_call" | custom-call | tf_op jit(solution)/shard_map/pallas_call | solution.py:623
